TPU v7x, 128 devices: a whole 4x4x4 slice. The times are simulated.
128 devices in a mesh: gx: 8 (over y, core), gy: 16 (over z, x).
Axes of the slice: x: 4, y: 4, z: 4, core: 2. Of those that a mesh axis runs over, the one named last changes fastest.
Arguments:
- fine_list: int32 [16384], P(('gx', 'gy')), may hold values from -1 to 12287, as said below
- fine_residual: float32 [16384, 6, 192], P(('gx', 'gy')), may hold values from -6 to 6
- solid_bits: int32 [16384, 3], P(('gx', 'gy')), may hold values from 0 to 1073741823
- restrict_ops: float32 [8, 192, 192], replicated, may hold values from -0.4375 to 0.4375
- operator: bfloat16 [8, 16, 12, 27, 192, 192], P('gx', 'gy'), as said below
- pattern: int32 [8, 16, 12, 26], P('gx', 'gy'), may hold values from 0 to 25, each once within a row
Outputs:
- fine_correction: float32 [16384, 6, 192], P(('gx', 'gy'))
- coarse_solution: float32 [8, 16, 12, 6, 192], P('gx', 'gy')
Inputs may be any that keep to these rules, and one draw needn't show every extreme that they name: `fine_list`: an entry 8 c + o names coarse brick c and octant o; -1 marks an empty slot. Every live entry of a device names a coarse brick owned by that device or by one of the devices next to it along gx, gy or both, the owner of brick (X, Y, Z) being the device with index X // 1 along gx and Y // 1 along gy. `operator`: block 0 of each row is the brick's own block; the other 26 blocks act on the neighbours in the order that pattern gives. The own blocks' diagonal entries are at least 0.6.
All inputs are finite; a program needn't handle non-finite values.
Results may differ from a plain program's by a relative error of at most 0.015.
Values may be sent and summed in bfloat16 or wider, within the bound.
A program may use at most 128 MiB of HBM per device.

v0:
```python
import jax
import jax.numpy as jnp
import numpy as np
from jax import lax
from jax.sharding import PartitionSpec as P

SWEEPS = 8


damping = 0.8


def extended(cells, sides, width):
    for axis, dim in sides:
        count = lax.axis_size(axis)
        ends = count - 1
        head = lax.slice_in_dim(cells, 0, width, axis=dim)
        tail = lax.slice_in_dim(cells, cells.shape[dim] - width, cells.shape[dim], axis=dim)
        cells = jnp.concatenate(
            [
                lax.ppermute(tail, axis, [(i, (i + 1) % count) for i in range(ends)]),
                cells,
                lax.ppermute(head, axis, [((i + 1) % count, i) for i in range(ends)]),
            ],
            axis=dim,
        )
    return cells


def shortened(value):
    return jax.tree.map(lambda a: a.astype(jnp.bfloat16) if a.dtype == jnp.float32 else a, value)


def value_mask(solid_bits, brick_values):
    node_count = brick_values // 3
    node_ids = np.arange(node_count)
    word_values = solid_bits[:, node_ids // 30]
    shifts = jnp.asarray(node_ids % 30, dtype=jnp.int32)
    node_flags = jnp.bitwise_and(jnp.right_shift(word_values, shifts[None, :]), 1).astype(
        jnp.float32
    )
    return jnp.concatenate([node_flags, node_flags, node_flags], axis=1)


def neighbour_index(pattern, span_x, span_y, span_z):
    offset = pattern + (pattern >= 13).astype(jnp.int32)
    own_zero = jnp.zeros((span_x, span_y, span_z, 1), jnp.int32)
    step_x = jnp.concatenate([own_zero, offset // 9 - 1], axis=3)
    step_y = jnp.concatenate([own_zero, offset // 3 % 3 - 1], axis=3)
    step_z = jnp.concatenate([own_zero, offset % 3 - 1], axis=3)
    base_x = lax.broadcasted_iota(jnp.int32, (span_x, span_y, span_z, 1), 0)
    base_y = lax.broadcasted_iota(jnp.int32, (span_x, span_y, span_z, 1), 1)
    base_z = lax.broadcasted_iota(jnp.int32, (span_x, span_y, span_z, 1), 2)
    return ((base_x + 1 + step_x) * (span_y + 2) + (base_y + 1 + step_y)) * (span_z + 2) + (
        base_z + 1 + step_z
    )


def octant_apply(rows_in, octant, restrict_ops, transpose):
    einsum_form = "oji,klj->okli" if transpose else "oij,klj->okli"
    every_octant = jnp.einsum(einsum_form, restrict_ops, rows_in, precision=lax.Precision.HIGHEST)
    selector = (octant[None, :] == jnp.arange(8, dtype=jnp.int32)[:, None]).astype(jnp.float32)
    return jnp.sum(every_octant * selector[:, :, None, None], axis=0)


def surround(rounded):
    padded = extended(rounded, (("gx", 0), ("gy", 1)), 1)
    padded = jnp.pad(padded, ((0, 0), (0, 0), (1, 1), (0, 0), (0, 0)))
    return padded.reshape(-1, padded.shape[3], padded.shape[4])


def local(fine_list, fine_residual, solid_bits, restrict_ops, operator, pattern):
    brick_values = restrict_ops.shape[1]
    load_cases = fine_residual.shape[1]
    span_x, span_y, span_z = (operator.shape[0], operator.shape[1], operator.shape[2])
    grid_y = lax.axis_size("gy")
    whole_y = span_y * grid_y
    bricks_here = span_x * span_y * span_z
    here_x = lax.axis_index("gx")
    here_y = lax.axis_index("gy")
    occupied = fine_list >= 0
    coarse_id = jnp.where(occupied, fine_list // 8, 0)
    octant = fine_list % 8
    pos_x = coarse_id // (whole_y * span_z)
    pos_y = coarse_id // span_z % whole_y
    pos_z = coarse_id % span_z
    step_x = pos_x // span_x - here_x
    step_y = pos_y // span_y - here_y
    local_x = pos_x % span_x
    local_y = pos_y % span_y
    local_id = (local_x * span_y + local_y) * span_z + pos_z
    fine_mask = value_mask(solid_bits, brick_values) * occupied[:, None].astype(jnp.float32)
    masked = fine_residual * fine_mask[:, None, :]
    restricted = octant_apply(masked, octant, restrict_ops, False)
    dest_id = jnp.where(occupied, ((step_x + 1) * 3 + step_y + 1) * bricks_here + local_id, -1)
    packer = (dest_id[None, :] == jnp.arange(9 * bricks_here, dtype=jnp.int32)[:, None]).astype(
        jnp.float32
    )
    outgoing = jnp.einsum("dk,klv->dlv", packer, restricted, precision=lax.Precision.HIGHEST)
    outgoing = outgoing.reshape(3, 3, span_x, span_y, span_z, load_cases, brick_values)
    padded = extended(outgoing.astype(jnp.bfloat16), (("gx", 0), ("gy", 1)), 1).astype(
        outgoing.dtype
    )
    coarse_rhs = jnp.sum(padded[0::2, 0::2], axis=(0, 1))
    diag_values = jnp.diagonal(operator[:, :, :, 0], axis1=-2, axis2=-1).astype(jnp.float32)
    step_scale = damping / diag_values[:, :, :, None, :]
    coarse_solution = step_scale * coarse_rhs
    row_index = neighbour_index(pattern, span_x, span_y, span_z)
    for step_index in range(SWEEPS - 1):
        rounded = coarse_solution.astype(jnp.bfloat16)
        flat_rows = surround(rounded)
        beside_all = flat_rows[row_index]
        applied = jnp.einsum(
            "xyzkij,xyzklj->xyzli", operator, beside_all, preferred_element_type=jnp.float32
        )
        coarse_solution = coarse_solution + step_scale * (coarse_rhs - applied)
    beside = extended(shortened(coarse_solution), (("gx", 0), ("gy", 1)), span_x).astype(
        coarse_solution.dtype
    )
    beside_rows = beside.reshape(-1, load_cases, brick_values)
    fetch_row = (
        ((step_x + 1) * span_x + local_x) * (3 * span_y) + (step_y + 1) * span_y + local_y
    ) * span_z + pos_z
    fetch_row = jnp.where(occupied, fetch_row, 0)
    fetched = beside_rows[fetch_row]
    fine_correction = octant_apply(fetched, octant, restrict_ops, True) * fine_mask[:, None, :]
    return (fine_correction, coarse_solution)


def solution(mesh):
    in_specs = (
        P(("gx", "gy")),
        P(("gx", "gy"), None, None),
        P(("gx", "gy"), None),
        P(),
        P("gx", "gy", None, None, None, None),
        P("gx", "gy", None, None),
    )
    out_specs = (P(("gx", "gy"), None, None), P("gx", "gy", None, None, None))
    return jax.shard_map(local, mesh=mesh, in_specs=in_specs, out_specs=out_specs, check_vma=False)
```

profile of v0, /device:TPU:105, one launch (start us, length us, event | category | flops | bytes accessed | tf_op | source)
XLA Modules:
  0.0 307.7 jit_solution(12628552271800486206)
XLA Ops:
  5.5 5.5 %fusion.15 = f32[128,6,192]{0,2,1:T(8,128)S(1)} fusion(f32[8,128]{1,0:T(8,128)S(1)} %fusion.123, f32[8,192,192]{2,1,0:T(8,128)S(1)} %copy-done, f32[128,6,192]{0,2,1:T(8,128)} %param.10, f32[128,192]{0,1:T(8,128)S(1)} %maximum_multiply_fusion), kind=kOutput, calls=%fused_computation.27 | convolution fusion | flops 2720268288 | bytes 2461696 | tf_op jit(solution)/shard_map/oij,klj->okli/dot_general | solution.py:61
  18.3 6.6 %copy.93 = bf16[1,1,12,1,192,192]{2,5,4,3,1,0:T(8,128)(2,1)} copy(bf16[1,1,12,1,192,192]{5,4,3,2,1,0:T(8,128)(2,1)S(1)} %slice-done) | data formatting | bytes 1769472
  25.0 5.4 %gather_fusion = bf16[192,12]{1,0:T(8,128)(2,1)S(1)} fusion(bf16[12,192,192]{0,2,1:T(8,128)(2,1)} %bitcast.217, s32[192]{0:T(256)S(1)} %bitcast.218), kind=kCustom, calls=%fused_computation | custom fusion | bytes 10752 | tf_op jit(solution)/shard_map/jit(diagonal)/gather | solution.py:105
  30.6 3.1 %collective-permute-start.2 = (bf16[5,1,1,1,12,6,192]{6,4,5,1,0,3,2:T(8,128)(2,1)S(1)}, bf16[5,1,1,1,12,6,192]{6,4,5,1,0,3,2:T(8,128)(2,1)S(1)}, u32[]{:S(2)}, u32[]{:S(2)}) collective-permute-start(bf16[5,1,1,1,12,6,192]{6,4,5,1,0,3,2:T(8,128)(2,1)S(1)} %get-tuple-element.16), channel_id=1, source_target_pairs={{0,1},{1,2},{2,3},{3,4},{4,5},{5,6},{6,7},{7,8},{8,9},{9,10},{10,1... | collective-permute-start | bytes 414728 | tf_op jit(solution)/shard_map/ppermute | solution.py:21
  33.7 4.3 %collective-permute-start.3 = (bf16[5,1,1,1,12,6,192]{6,4,5,1,0,3,2:T(8,128)(2,1)S(1)}, bf16[5,1,1,1,12,6,192]{6,4,5,1,0,3,2:T(8,128)(2,1)S(1)}, u32[]{:S(2)}, u32[]{:S(2)}) collective-permute-start(bf16[5,1,1,1,12,6,192]{6,4,5,1,0,3,2:T(8,128)(2,1)S(1)} %get-tuple-element.17), channel_id=1, source_target_pairs={{1,0},{2,1},{3,2},{4,3},{5,4},{6,5},{7,6},{8,7},{9,8},{10,9},{11,1... | collective-permute-start | bytes 414728 | tf_op jit(solution)/shard_map/ppermute | solution.py:23
  38.2 3.9 %collective-permute-done.2 = bf16[5,1,1,1,12,6,192]{6,4,5,1,0,3,2:T(8,128)(2,1)S(1)} collective-permute-done((bf16[5,1,1,1,12,6,192]{6,4,5,1,0,3,2:T(8,128)(2,1)S(1)}, bf16[5,1,1,1,12,6,192]{6,4,5,1,0,3,2:T(8,128)(2,1)S(1)}, u32[]{:S(2)}, u32[]{:S(2)}) %collective-permute-start.2) | collective-permute-done | bytes 138272 | tf_op jit(solution)/shard_map/ppermute | solution.py:21
  44.1 3.4 %collective-permute-start.4 = (bf16[1,1,12,6,192]{4,2,3,1,0:T(8,128)(2,1)S(1)}, bf16[1,1,12,6,192]{4,2,3,1,0:T(8,128)(2,1)S(1)}, u32[]{:S(2)}, u32[]{:S(2)}) collective-permute-start(bf16[1,1,12,6,192]{4,2,3,1,0:T(8,128)(2,1)S(1)} %fusion.113), channel_id=1, source_target_pairs={{0,16},{16,32},{32,48},{48,64},{64,80},{80,96},{96,112},{1,17},{17... | collective-permute-start | bytes 82952 | tf_op jit(solution)/shard_map/ppermute | solution.py:21
  49.7 3.3 %collective-permute-done.5 = bf16[1,1,12,6,192]{4,2,3,1,0:T(8,128)(2,1)S(1)} collective-permute-done((bf16[1,1,12,6,192]{4,2,3,1,0:T(8,128)(2,1)S(1)}, bf16[1,1,12,6,192]{4,2,3,1,0:T(8,128)(2,1)S(1)}, u32[]{:S(2)}, u32[]{:S(2)}) %collective-permute-start.5) | collective-permute-done | bytes 27680 | tf_op jit(solution)/shard_map/ppermute | solution.py:23
  56.0 5.2 %collective-permute-start.7 = (bf16[3,1,12,6,192]{4,2,3,1,0:T(8,128)(2,1)S(1)}, bf16[3,1,12,6,192]{4,2,3,1,0:T(8,128)(2,1)S(1)}, u32[]{:S(2)}, u32[]{:S(2)}) collective-permute-start(bf16[3,1,12,6,192]{4,2,3,1,0:T(8,128)(2,1)S(1)} %pad_maximum_fusion.6), channel_id=1, source_target_pairs={{1,0},{2,1},{3,2},{4,3},{5,4},{6,5},{7,6},{8,7},{9,8},{10,9},{11,1... | collective-permute-start | bytes 248840 | tf_op jit(solution)/shard_map/ppermute | solution.py:23
  66.2 13.8 %fusion.99 = f32[12,6,192]{2,1,0:T(8,128)S(1)} fusion(bf16[12,27,6,192]{3,2,1,0:T(8,128)(2,1)S(1)} %bitcast.234, bf16[1,1,12,27,192,192]{5,4,3,2,1,0:T(8,128)(2,1)} %param.13, f32[12,6,192]{2,0,1:T(8,128)S(1)} %convert_reduce_fusion, f32[12,192]{1,0:T(8,128)S(1)} %copy.58), kind=kOutput, calls=%fused_computation.61 | convolution fusion | flops 143368704 | bytes 24754176 | tf_op jit(solution)/shard_map/xyzkij,xyzklj->xyzli/dot_general | solution.py:113
  84.4 3.5 %collective-permute-done.9 = bf16[1,1,12,6,192]{4,3,2,1,0:T(8,128)(2,1)S(1)} collective-permute-done((bf16[1,1,12,6,192]{4,3,2,1,0:T(8,128)(2,1)S(1)}, bf16[1,1,12,6,192]{4,3,2,1,0:T(8,128)(2,1)S(1)}, u32[]{:S(2)}, u32[]{:S(2)}) %collective-permute-start.9) | collective-permute-done | bytes 27680 | tf_op jit(solution)/shard_map/ppermute | solution.py:23
  89.8 6.2 %collective-permute-start.11 = (bf16[3,1,12,6,192]{4,3,2,1,0:T(8,128)(2,1)S(1)}, bf16[3,1,12,6,192]{4,3,2,1,0:T(8,128)(2,1)S(1)}, u32[]{:S(2)}, u32[]{:S(2)}) collective-permute-start(bf16[3,1,12,6,192]{4,3,2,1,0:T(8,128)(2,1)S(1)} %pad_maximum_fusion.7), channel_id=1, source_target_pairs={{1,0},{2,1},{3,2},{4,3},{5,4},{6,5},{7,6},{8,7},{9,8},{10,9},{11,1... | collective-permute-start | bytes 248840 | tf_op jit(solution)/shard_map/ppermute | solution.py:23
  101.3 13.9 %fusion.90 = f32[12,6,192]{2,1,0:T(8,128)S(1)} fusion(f32[12,6,192]{2,1,0:T(8,128)} %copy-done.1, bf16[12,27,6,192]{3,2,1,0:T(8,128)(2,1)S(1)} %bitcast.229, bf16[1,1,12,27,192,192]{5,4,3,2,1,0:T(8,128)(2,1)} %param.13, f32[12,6,192]{2,0,1:T(8,128)S(1)} %convert_reduce_fusion, f32[12,192]{1,0:T(8,128)S(1)} %copy.58), kind=kOutput, calls=%fused_computation.58 | convolution fusion | flops 143368704 | bytes 24809472 | tf_op jit(solution)/shard_map/xyzkij,xyzklj->xyzli/dot_general | solution.py:113
  124.5 6.2 %collective-permute-start.15 = (bf16[3,1,12,6,192]{4,3,2,1,0:T(8,128)(2,1)S(1)}, bf16[3,1,12,6,192]{4,3,2,1,0:T(8,128)(2,1)S(1)}, u32[]{:S(2)}, u32[]{:S(2)}) collective-permute-start(bf16[3,1,12,6,192]{4,3,2,1,0:T(8,128)(2,1)S(1)} %pad_maximum_fusion.8), channel_id=1, source_target_pairs={{1,0},{2,1},{3,2},{4,3},{5,4},{6,5},{7,6},{8,7},{9,8},{10,9},{11,1... | collective-permute-start | bytes 248840 | tf_op jit(solution)/shard_map/ppermute | solution.py:23
  135.3 13.9 %fusion.81 = f32[12,6,192]{2,1,0:T(8,128)S(1)} fusion(f32[12,6,192]{2,1,0:T(8,128)} %copy-done.3, bf16[12,27,6,192]{3,2,1,0:T(8,128)(2,1)S(1)} %bitcast.230, bf16[1,1,12,27,192,192]{5,4,3,2,1,0:T(8,128)(2,1)} %param.13, f32[12,6,192]{2,0,1:T(8,128)S(1)} %convert_reduce_fusion, f32[12,192]{1,0:T(8,128)S(1)} %copy.58), kind=kOutput, calls=%fused_computation.55 | convolution fusion | flops 143368704 | bytes 24809472 | tf_op jit(solution)/shard_map/xyzkij,xyzklj->xyzli/dot_general | solution.py:113
  158.6 6.2 %collective-permute-start.19 = (bf16[3,1,12,6,192]{4,3,2,1,0:T(8,128)(2,1)S(1)}, bf16[3,1,12,6,192]{4,3,2,1,0:T(8,128)(2,1)S(1)}, u32[]{:S(2)}, u32[]{:S(2)}) collective-permute-start(bf16[3,1,12,6,192]{4,3,2,1,0:T(8,128)(2,1)S(1)} %pad_maximum_fusion.9), channel_id=1, source_target_pairs={{1,0},{2,1},{3,2},{4,3},{5,4},{6,5},{7,6},{8,7},{9,8},{10,9},{11,1... | collective-permute-start | bytes 248840 | tf_op jit(solution)/shard_map/ppermute | solution.py:23
  168.7 13.9 %fusion.72 = f32[12,6,192]{2,1,0:T(8,128)S(1)} fusion(f32[12,6,192]{2,1,0:T(8,128)} %copy-done.4, bf16[12,27,6,192]{3,2,1,0:T(8,128)(2,1)S(1)} %bitcast.231, bf16[1,1,12,27,192,192]{5,4,3,2,1,0:T(8,128)(2,1)} %param.13, f32[12,6,192]{2,0,1:T(8,128)S(1)} %convert_reduce_fusion, f32[12,192]{1,0:T(8,128)S(1)} %copy.58), kind=kOutput, calls=%fused_computation.52 | convolution fusion | flops 143368704 | bytes 24809472 | tf_op jit(solution)/shard_map/xyzkij,xyzklj->xyzli/dot_general | solution.py:113
  192.7 6.2 %collective-permute-start.23 = (bf16[3,1,12,6,192]{4,3,2,1,0:T(8,128)(2,1)S(1)}, bf16[3,1,12,6,192]{4,3,2,1,0:T(8,128)(2,1)S(1)}, u32[]{:S(2)}, u32[]{:S(2)}) collective-permute-start(bf16[3,1,12,6,192]{4,3,2,1,0:T(8,128)(2,1)S(1)} %pad_maximum_fusion.10), channel_id=1, source_target_pairs={{1,0},{2,1},{3,2},{4,3},{5,4},{6,5},{7,6},{8,7},{9,8},{10,9},{11,1... | collective-permute-start | bytes 248840 | tf_op jit(solution)/shard_map/ppermute | solution.py:23
  202.8 13.9 %fusion.63 = f32[12,6,192]{2,1,0:T(8,128)S(1)} fusion(f32[12,6,192]{2,1,0:T(8,128)} %copy-done.5, bf16[12,27,6,192]{3,2,1,0:T(8,128)(2,1)S(1)} %bitcast.232, bf16[1,1,12,27,192,192]{5,4,3,2,1,0:T(8,128)(2,1)} %param.13, f32[12,6,192]{2,0,1:T(8,128)S(1)} %convert_reduce_fusion, f32[12,192]{1,0:T(8,128)S(1)} %copy.58), kind=kOutput, calls=%fused_computation.49 | convolution fusion | flops 143368704 | bytes 24809472 | tf_op jit(solution)/shard_map/xyzkij,xyzklj->xyzli/dot_general | solution.py:113
  226.8 6.2 %collective-permute-start.27 = (bf16[3,1,12,6,192]{4,3,2,1,0:T(8,128)(2,1)S(1)}, bf16[3,1,12,6,192]{4,3,2,1,0:T(8,128)(2,1)S(1)}, u32[]{:S(2)}, u32[]{:S(2)}) collective-permute-start(bf16[3,1,12,6,192]{4,3,2,1,0:T(8,128)(2,1)S(1)} %pad_maximum_fusion.11), channel_id=1, source_target_pairs={{1,0},{2,1},{3,2},{4,3},{5,4},{6,5},{7,6},{8,7},{9,8},{10,9},{11,1... | collective-permute-start | bytes 248840 | tf_op jit(solution)/shard_map/ppermute | solution.py:23
  236.9 13.9 %fusion.54 = f32[12,6,192]{2,1,0:T(8,128)S(1)} fusion(f32[12,6,192]{2,1,0:T(8,128)} %copy-done.6, bf16[12,27,6,192]{3,2,1,0:T(8,128)(2,1)S(1)} %bitcast.233, bf16[1,1,12,27,192,192]{5,4,3,2,1,0:T(8,128)(2,1)} %param.13, f32[12,6,192]{2,0,1:T(8,128)S(1)} %convert_reduce_fusion, f32[12,192]{1,0:T(8,128)S(1)} %copy.58), kind=kOutput, calls=%fused_computation.46 | convolution fusion | flops 143368704 | bytes 24809472 | tf_op jit(solution)/shard_map/xyzkij,xyzklj->xyzli/dot_general | solution.py:113
  260.9 6.2 %collective-permute-start.31 = (bf16[3,1,12,6,192]{4,3,2,1,0:T(8,128)(2,1)S(1)}, bf16[3,1,12,6,192]{4,3,2,1,0:T(8,128)(2,1)S(1)}, u32[]{:S(2)}, u32[]{:S(2)}) collective-permute-start(bf16[3,1,12,6,192]{4,3,2,1,0:T(8,128)(2,1)S(1)} %pad_maximum_fusion.12), channel_id=1, source_target_pairs={{1,0},{2,1},{3,2},{4,3},{5,4},{6,5},{7,6},{8,7},{9,8},{10,9},{11,1... | collective-permute-start | bytes 248840 | tf_op jit(solution)/shard_map/ppermute | solution.py:23
  271.0 13.9 %fusion.45 = f32[12,6,192]{2,1,0:T(8,128)S(1)} fusion(f32[12,6,192]{2,1,0:T(8,128)} %copy-done.2, bf16[12,27,6,192]{3,2,1,0:T(8,128)(2,1)S(1)} %bitcast.228, bf16[1,1,12,27,192,192]{5,4,3,2,1,0:T(8,128)(2,1)} %param.13, f32[12,6,192]{2,0,1:T(8,128)S(1)} %convert_reduce_fusion, f32[12,192]{1,0:T(8,128)S(1)} %copy.58), kind=kOutput, calls=%fused_computation.43 | convolution fusion | flops 143368704 | bytes 24809472 | tf_op jit(solution)/shard_map/xyzkij,xyzklj->xyzli/dot_general | solution.py:113
  295.0 6.2 %collective-permute-start.35 = (bf16[3,1,12,6,192]{4,3,2,1,0:T(8,128)(2,1)S(1)}, bf16[3,1,12,6,192]{4,3,2,1,0:T(8,128)(2,1)S(1)}, u32[]{:S(2)}, u32[]{:S(2)}) collective-permute-start(bf16[3,1,12,6,192]{4,3,2,1,0:T(8,128)(2,1)S(1)} %pad_maximum_fusion.13), channel_id=1, source_target_pairs={{1,0},{2,1},{3,2},{4,3},{5,4},{6,5},{7,6},{8,7},{9,8},{10,9},{11,1... | collective-permute-start | bytes 248840 | tf_op jit(solution)/shard_map/ppermute | solution.py:23
  (140 shorter events, 121.8 us)
Async XLA Ops:
  12.5 17.9 %collective-permute-start.1 = (bf16[1,3,1,1,12,6,192]{6,4,5,1,3,2,0:T(8,128)(2,1)}, bf16[1,3,1,1,12,6,192]{6,4,5,1,3,2,0:T(8,128)(2,1)S(1)}, u32[]{:S(2)}, u32[]{:S(2)}) collective-permute-start(bf16[1,3,1,1,12,6,192]{6,4,5,1,3,2,0:T(8,128)(2,1)} %get-tuple-element.19), channel_id=1, source_target_pairs={{16,0},{32,16},{48,32},{64,48},{80,64},{96,80},{112,96},{17,1},{33... | collective-permute-start | bytes 248840 | tf_op jit(solution)/shard_map/ppermute | solution.py:23
  15.2 15.2 %collective-permute-start = (bf16[1,3,1,1,12,6,192]{6,4,5,1,0,3,2:T(8,128)(2,1)}, bf16[1,3,1,1,12,6,192]{6,4,5,1,0,3,2:T(8,128)(2,1)S(1)}, u32[]{:S(2)}, u32[]{:S(2)}) collective-permute-start(bf16[1,3,1,1,12,6,192]{6,4,5,1,0,3,2:T(8,128)(2,1)} %get-tuple-element.18), channel_id=1, source_target_pairs={{0,16},{16,32},{32,48},{48,64},{64,80},{80,96},{96,112},{1,17},{17... | collective-permute-start | bytes 248840 | tf_op jit(solution)/shard_map/ppermute | solution.py:21
  30.6 11.5 %collective-permute-start.2 = (bf16[5,1,1,1,12,6,192]{6,4,5,1,0,3,2:T(8,128)(2,1)S(1)}, bf16[5,1,1,1,12,6,192]{6,4,5,1,0,3,2:T(8,128)(2,1)S(1)}, u32[]{:S(2)}, u32[]{:S(2)}) collective-permute-start(bf16[5,1,1,1,12,6,192]{6,4,5,1,0,3,2:T(8,128)(2,1)S(1)} %get-tuple-element.16), channel_id=1, source_target_pairs={{0,1},{1,2},{2,3},{3,4},{4,5},{5,6},{6,7},{7,8},{8,9},{9,10},{10,1... | collective-permute-start | bytes 414728 | tf_op jit(solution)/shard_map/ppermute | solution.py:21
  33.7 10.0 %collective-permute-start.3 = (bf16[5,1,1,1,12,6,192]{6,4,5,1,0,3,2:T(8,128)(2,1)S(1)}, bf16[5,1,1,1,12,6,192]{6,4,5,1,0,3,2:T(8,128)(2,1)S(1)}, u32[]{:S(2)}, u32[]{:S(2)}) collective-permute-start(bf16[5,1,1,1,12,6,192]{6,4,5,1,0,3,2:T(8,128)(2,1)S(1)} %get-tuple-element.17), channel_id=1, source_target_pairs={{1,0},{2,1},{3,2},{4,3},{5,4},{6,5},{7,6},{8,7},{9,8},{10,9},{11,1... | collective-permute-start | bytes 414728 | tf_op jit(solution)/shard_map/ppermute | solution.py:23
  53.0 9.4 %collective-permute-start.6 = (bf16[3,1,12,6,192]{4,2,3,1,0:T(8,128)(2,1)S(1)}, bf16[3,1,12,6,192]{4,2,3,1,0:T(8,128)(2,1)S(1)}, u32[]{:S(2)}, u32[]{:S(2)}) collective-permute-start(bf16[3,1,12,6,192]{4,2,3,1,0:T(8,128)(2,1)S(1)} %pad_maximum_fusion.6), channel_id=1, source_target_pairs={{0,1},{1,2},{2,3},{3,4},{4,5},{5,6},{6,7},{7,8},{8,9},{9,10},{10,1... | collective-permute-start | bytes 248840 | tf_op jit(solution)/shard_map/ppermute | solution.py:21
  56.0 8.2 %collective-permute-start.7 = (bf16[3,1,12,6,192]{4,2,3,1,0:T(8,128)(2,1)S(1)}, bf16[3,1,12,6,192]{4,2,3,1,0:T(8,128)(2,1)S(1)}, u32[]{:S(2)}, u32[]{:S(2)}) collective-permute-start(bf16[3,1,12,6,192]{4,2,3,1,0:T(8,128)(2,1)S(1)} %pad_maximum_fusion.6), channel_id=1, source_target_pairs={{1,0},{2,1},{3,2},{4,3},{5,4},{6,5},{7,6},{8,7},{9,8},{10,9},{11,1... | collective-permute-start | bytes 248840 | tf_op jit(solution)/shard_map/ppermute | solution.py:23
  87.9 9.8 %collective-permute-start.10 = (bf16[3,1,12,6,192]{4,3,2,1,0:T(8,128)(2,1)S(1)}, bf16[3,1,12,6,192]{4,3,2,1,0:T(8,128)(2,1)S(1)}, u32[]{:S(2)}, u32[]{:S(2)}) collective-permute-start(bf16[3,1,12,6,192]{4,3,2,1,0:T(8,128)(2,1)S(1)} %pad_maximum_fusion.7), channel_id=1, source_target_pairs={{0,1},{1,2},{2,3},{3,4},{4,5},{5,6},{6,7},{7,8},{8,9},{9,10},{10,1... | collective-permute-start | bytes 248840 | tf_op jit(solution)/shard_map/ppermute | solution.py:21
  89.8 9.6 %collective-permute-start.11 = (bf16[3,1,12,6,192]{4,3,2,1,0:T(8,128)(2,1)S(1)}, bf16[3,1,12,6,192]{4,3,2,1,0:T(8,128)(2,1)S(1)}, u32[]{:S(2)}, u32[]{:S(2)}) collective-permute-start(bf16[3,1,12,6,192]{4,3,2,1,0:T(8,128)(2,1)S(1)} %pad_maximum_fusion.7), channel_id=1, source_target_pairs={{1,0},{2,1},{3,2},{4,3},{5,4},{6,5},{7,6},{8,7},{9,8},{10,9},{11,1... | collective-permute-start | bytes 248840 | tf_op jit(solution)/shard_map/ppermute | solution.py:23
  122.5 9.9 %collective-permute-start.14 = (bf16[3,1,12,6,192]{4,3,2,1,0:T(8,128)(2,1)S(1)}, bf16[3,1,12,6,192]{4,3,2,1,0:T(8,128)(2,1)S(1)}, u32[]{:S(2)}, u32[]{:S(2)}) collective-permute-start(bf16[3,1,12,6,192]{4,3,2,1,0:T(8,128)(2,1)S(1)} %pad_maximum_fusion.8), channel_id=1, source_target_pairs={{0,1},{1,2},{2,3},{3,4},{4,5},{5,6},{6,7},{7,8},{8,9},{9,10},{10,1... | collective-permute-start | bytes 248840 | tf_op jit(solution)/shard_map/ppermute | solution.py:21
  124.5 9.0 %collective-permute-start.15 = (bf16[3,1,12,6,192]{4,3,2,1,0:T(8,128)(2,1)S(1)}, bf16[3,1,12,6,192]{4,3,2,1,0:T(8,128)(2,1)S(1)}, u32[]{:S(2)}, u32[]{:S(2)}) collective-permute-start(bf16[3,1,12,6,192]{4,3,2,1,0:T(8,128)(2,1)S(1)} %pad_maximum_fusion.8), channel_id=1, source_target_pairs={{1,0},{2,1},{3,2},{4,3},{5,4},{6,5},{7,6},{8,7},{9,8},{10,9},{11,1... | collective-permute-start | bytes 248840 | tf_op jit(solution)/shard_map/ppermute | solution.py:23
  156.6 9.3 %collective-permute-start.18 = (bf16[3,1,12,6,192]{4,3,2,1,0:T(8,128)(2,1)S(1)}, bf16[3,1,12,6,192]{4,3,2,1,0:T(8,128)(2,1)S(1)}, u32[]{:S(2)}, u32[]{:S(2)}) collective-permute-start(bf16[3,1,12,6,192]{4,3,2,1,0:T(8,128)(2,1)S(1)} %pad_maximum_fusion.9), channel_id=1, source_target_pairs={{0,1},{1,2},{2,3},{3,4},{4,5},{5,6},{6,7},{7,8},{8,9},{9,10},{10,1... | collective-permute-start | bytes 248840 | tf_op jit(solution)/shard_map/ppermute | solution.py:21
  158.6 8.3 %collective-permute-start.19 = (bf16[3,1,12,6,192]{4,3,2,1,0:T(8,128)(2,1)S(1)}, bf16[3,1,12,6,192]{4,3,2,1,0:T(8,128)(2,1)S(1)}, u32[]{:S(2)}, u32[]{:S(2)}) collective-permute-start(bf16[3,1,12,6,192]{4,3,2,1,0:T(8,128)(2,1)S(1)} %pad_maximum_fusion.9), channel_id=1, source_target_pairs={{1,0},{2,1},{3,2},{4,3},{5,4},{6,5},{7,6},{8,7},{9,8},{10,9},{11,1... | collective-permute-start | bytes 248840 | tf_op jit(solution)/shard_map/ppermute | solution.py:23
  182.5 5.8 %collective-permute-start.20 = (bf16[1,1,12,6,192]{4,3,2,1,0:T(8,128)(2,1)S(1)}, bf16[1,1,12,6,192]{4,3,2,1,0:T(8,128)(2,1)S(1)}, u32[]{:S(2)}, u32[]{:S(2)}) collective-permute-start(bf16[1,1,12,6,192]{4,3,2,1,0:T(8,128)(2,1)S(1)} %convert_bitcast_fusion.3), channel_id=1, source_target_pairs={{0,16},{16,32},{32,48},{48,64},{64,80},{80,96},{96,112},{1,17},{17... | collective-permute-start | bytes 82952 | tf_op jit(solution)/shard_map/ppermute | solution.py:21
  190.8 9.3 %collective-permute-start.22 = (bf16[3,1,12,6,192]{4,3,2,1,0:T(8,128)(2,1)S(1)}, bf16[3,1,12,6,192]{4,3,2,1,0:T(8,128)(2,1)S(1)}, u32[]{:S(2)}, u32[]{:S(2)}) collective-permute-start(bf16[3,1,12,6,192]{4,3,2,1,0:T(8,128)(2,1)S(1)} %pad_maximum_fusion.10), channel_id=1, source_target_pairs={{0,1},{1,2},{2,3},{3,4},{4,5},{5,6},{6,7},{7,8},{8,9},{9,10},{10,1... | collective-permute-start | bytes 248840 | tf_op jit(solution)/shard_map/ppermute | solution.py:21
  192.7 8.3 %collective-permute-start.23 = (bf16[3,1,12,6,192]{4,3,2,1,0:T(8,128)(2,1)S(1)}, bf16[3,1,12,6,192]{4,3,2,1,0:T(8,128)(2,1)S(1)}, u32[]{:S(2)}, u32[]{:S(2)}) collective-permute-start(bf16[3,1,12,6,192]{4,3,2,1,0:T(8,128)(2,1)S(1)} %pad_maximum_fusion.10), channel_id=1, source_target_pairs={{1,0},{2,1},{3,2},{4,3},{5,4},{6,5},{7,6},{8,7},{9,8},{10,9},{11,1... | collective-permute-start | bytes 248840 | tf_op jit(solution)/shard_map/ppermute | solution.py:23
  216.7 5.8 %collective-permute-start.24 = (bf16[1,1,12,6,192]{4,3,2,1,0:T(8,128)(2,1)S(1)}, bf16[1,1,12,6,192]{4,3,2,1,0:T(8,128)(2,1)S(1)}, u32[]{:S(2)}, u32[]{:S(2)}) collective-permute-start(bf16[1,1,12,6,192]{4,3,2,1,0:T(8,128)(2,1)S(1)} %convert_bitcast_fusion.2), channel_id=1, source_target_pairs={{0,16},{16,32},{32,48},{48,64},{64,80},{80,96},{96,112},{1,17},{17... | collective-permute-start | bytes 82952 | tf_op jit(solution)/shard_map/ppermute | solution.py:21
  224.9 9.3 %collective-permute-start.26 = (bf16[3,1,12,6,192]{4,3,2,1,0:T(8,128)(2,1)S(1)}, bf16[3,1,12,6,192]{4,3,2,1,0:T(8,128)(2,1)S(1)}, u32[]{:S(2)}, u32[]{:S(2)}) collective-permute-start(bf16[3,1,12,6,192]{4,3,2,1,0:T(8,128)(2,1)S(1)} %pad_maximum_fusion.11), channel_id=1, source_target_pairs={{0,1},{1,2},{2,3},{3,4},{4,5},{5,6},{6,7},{7,8},{8,9},{9,10},{10,1... | collective-permute-start | bytes 248840 | tf_op jit(solution)/shard_map/ppermute | solution.py:21
  226.8 8.3 %collective-permute-start.27 = (bf16[3,1,12,6,192]{4,3,2,1,0:T(8,128)(2,1)S(1)}, bf16[3,1,12,6,192]{4,3,2,1,0:T(8,128)(2,1)S(1)}, u32[]{:S(2)}, u32[]{:S(2)}) collective-permute-start(bf16[3,1,12,6,192]{4,3,2,1,0:T(8,128)(2,1)S(1)} %pad_maximum_fusion.11), channel_id=1, source_target_pairs={{1,0},{2,1},{3,2},{4,3},{5,4},{6,5},{7,6},{8,7},{9,8},{10,9},{11,1... | collective-permute-start | bytes 248840 | tf_op jit(solution)/shard_map/ppermute | solution.py:23
  250.8 5.8 %collective-permute-start.28 = (bf16[1,1,12,6,192]{4,3,2,1,0:T(8,128)(2,1)S(1)}, bf16[1,1,12,6,192]{4,3,2,1,0:T(8,128)(2,1)S(1)}, u32[]{:S(2)}, u32[]{:S(2)}) collective-permute-start(bf16[1,1,12,6,192]{4,3,2,1,0:T(8,128)(2,1)S(1)} %convert_bitcast_fusion.1), channel_id=1, source_target_pairs={{0,16},{16,32},{32,48},{48,64},{64,80},{80,96},{96,112},{1,17},{17... | collective-permute-start | bytes 82952 | tf_op jit(solution)/shard_map/ppermute | solution.py:21
  259.0 9.3 %collective-permute-start.30 = (bf16[3,1,12,6,192]{4,3,2,1,0:T(8,128)(2,1)S(1)}, bf16[3,1,12,6,192]{4,3,2,1,0:T(8,128)(2,1)S(1)}, u32[]{:S(2)}, u32[]{:S(2)}) collective-permute-start(bf16[3,1,12,6,192]{4,3,2,1,0:T(8,128)(2,1)S(1)} %pad_maximum_fusion.12), channel_id=1, source_target_pairs={{0,1},{1,2},{2,3},{3,4},{4,5},{5,6},{6,7},{7,8},{8,9},{9,10},{10,1... | collective-permute-start | bytes 248840 | tf_op jit(solution)/shard_map/ppermute | solution.py:21
  260.9 8.3 %collective-permute-start.31 = (bf16[3,1,12,6,192]{4,3,2,1,0:T(8,128)(2,1)S(1)}, bf16[3,1,12,6,192]{4,3,2,1,0:T(8,128)(2,1)S(1)}, u32[]{:S(2)}, u32[]{:S(2)}) collective-permute-start(bf16[3,1,12,6,192]{4,3,2,1,0:T(8,128)(2,1)S(1)} %pad_maximum_fusion.12), channel_id=1, source_target_pairs={{1,0},{2,1},{3,2},{4,3},{5,4},{6,5},{7,6},{8,7},{9,8},{10,9},{11,1... | collective-permute-start | bytes 248840 | tf_op jit(solution)/shard_map/ppermute | solution.py:23
  284.9 5.8 %collective-permute-start.32 = (bf16[1,1,12,6,192]{4,3,2,1,0:T(8,128)(2,1)S(1)}, bf16[1,1,12,6,192]{4,3,2,1,0:T(8,128)(2,1)S(1)}, u32[]{:S(2)}, u32[]{:S(2)}) collective-permute-start(bf16[1,1,12,6,192]{4,3,2,1,0:T(8,128)(2,1)S(1)} %convert_bitcast_fusion), channel_id=1, source_target_pairs={{0,16},{16,32},{32,48},{48,64},{64,80},{80,96},{96,112},{1,17},{17... | collective-permute-start | bytes 82952 | tf_op jit(solution)/shard_map/ppermute | solution.py:21
  293.1 9.3 %collective-permute-start.34 = (bf16[3,1,12,6,192]{4,3,2,1,0:T(8,128)(2,1)S(1)}, bf16[3,1,12,6,192]{4,3,2,1,0:T(8,128)(2,1)S(1)}, u32[]{:S(2)}, u32[]{:S(2)}) collective-permute-start(bf16[3,1,12,6,192]{4,3,2,1,0:T(8,128)(2,1)S(1)} %pad_maximum_fusion.13), channel_id=1, source_target_pairs={{0,1},{1,2},{2,3},{3,4},{4,5},{5,6},{6,7},{7,8},{8,9},{9,10},{10,1... | collective-permute-start | bytes 248840 | tf_op jit(solution)/shard_map/ppermute | solution.py:21
  295.0 8.3 %collective-permute-start.35 = (bf16[3,1,12,6,192]{4,3,2,1,0:T(8,128)(2,1)S(1)}, bf16[3,1,12,6,192]{4,3,2,1,0:T(8,128)(2,1)S(1)}, u32[]{:S(2)}, u32[]{:S(2)}) collective-permute-start(bf16[3,1,12,6,192]{4,3,2,1,0:T(8,128)(2,1)S(1)} %pad_maximum_fusion.13), channel_id=1, source_target_pairs={{1,0},{2,1},{3,2},{4,3},{5,4},{6,5},{7,6},{8,7},{9,8},{10,9},{11,1... | collective-permute-start | bytes 248840 | tf_op jit(solution)/shard_map/ppermute | solution.py:23
  (23 other events, 198.8 us)
where the time goes:
time: 314 us; the launch traced here: 308 us
  starting transfers between devices  120 us (38%)
  matrix products  106 us (34%)
  waiting for transfers between devices  45.8 us (15%)
  local copies, waits for them, and re-layouts  27.7 us (9%)
  other arithmetic  6.48 us (2%)
    dot_general x7, matrix products, local(): jnp.einsum('xyzkij,xyzklj->xyzli', operator, beside_all, preferred_elemen...  96.9 us
    ppermute x18, starting transfers between devices, extended(): lax.ppermute(head, axis, [((i + 1) % count, i) for i in range(ends)])  77.1 us
    ppermute x18, starting transfers between devices, extended(): lax.ppermute(tail, axis, [(i, (i + 1) % count) for i in range(ends)])  43.3 us
    ppermute x18, waiting for transfers between devices, extended(): lax.ppermute(head, axis, [((i + 1) % count, i) for i in range(ends)])  32.2 us
    ppermute x18, waiting for transfers between devices, extended(): lax.ppermute(tail, axis, [(i, (i + 1) % count) for i in range(ends)])  13.6 us
    gather x7, local copies, waits for them, and re-layouts, local(): beside_all = flat_rows[row_index]  11.9 us
    dot_general x2, matrix products, octant_apply(): jnp.einsum(einsum_form, restrict_ops, rows_in, precision=lax.Precision.HI...  8.19 us
    unnamed x23, local copies, waits for them, and re-layouts  7.52 us
  transfers between devices with their start and end apart: 36, of which 26 were waited for; matrix products, arithmetic and copies ran while one was open for 4% of the time, Pallas kernels for 0%

commit v1 on v0

v1 whole, which is shorter than its diff:
```python
import functools
import jax
import jax.numpy as jnp
from jax import lax
from jax.experimental import pallas as pl
from jax.experimental.pallas import tpu as pltpu
from jax.sharding import PartitionSpec as P

SWEEPS = 8
DAMPING = 0.8
OFFSETS = [(dx, dy) for dx in (-1, 0, 1) for dy in (-1, 0, 1)]
OWN = 4
SLOT = {d: (d if d < OWN else d - 1) for d in range(9) if d != OWN}
SLOT[OWN] = 8
ZERO = 9
JOINED = ((0, 1), (2, 3), (5, 6), (7, 8))
NT = (((1,), (1,)), ((), ()))
F32 = jnp.float32
BF16 = jnp.bfloat16


def dot(a, b):
    return jnp.dot(a, b, preferred_element_type=F32)


def dot_nt(a, b):
    return lax.dot_general(a, b, NT, preferred_element_type=F32)


def swapped(tile):
    return jnp.concatenate([tile[8:16], tile[0:8]], axis=0)


def kernel(
    list_hbm, bits_hbm, residual_hbm, restrict_hbm, operator_hbm, pattern_hbm,
    correction_ref, coarse_ref,
    list_v, bits_v, residual_v, restrict_v, own_v, pattern_v, inverse_v, inverse_s,
    packed, restrict_b, restrict_t, gather_v, rhs_own, rhs_send, rhs_land,
    land, turned, joined, solution_v, rhs_v, scale_v,
    small_sem, raw_sem, inverse_sem, rhs_sems, send_sems, recv_sems,
    *raw,
):
    bricks = len(raw)
    pairs = bricks // 2
    loads = residual_v.shape[0]
    values = restrict_v.shape[1]
    slots = list_v.shape[1]
    rows = bricks * 8
    count_x = lax.axis_size("gx")
    count_y = lax.axis_size("gy")
    here_x = lax.axis_index("gx")
    here_y = lax.axis_index("gy")

    small = [
        pltpu.make_async_copy(src, dst, small_sem.at[i])
        for i, (src, dst) in enumerate(
            [
                (pattern_hbm, pattern_v),
                (list_hbm, list_v),
                (bits_hbm, bits_v),
                (residual_hbm, residual_v),
                (restrict_hbm, restrict_v),
                (operator_hbm.at[:, 0], own_v),
            ]
        )
    ]
    for copy in small:
        copy.start()
    big = [
        pltpu.make_async_copy(operator_hbm.at[c, pl.ds(1, 26)], raw[c], raw_sem.at[c])
        for c in range(bricks)
    ]
    for copy in big:
        copy.start()

    targets = []
    inside = []
    for d, (dx, dy) in enumerate(OFFSETS):
        to_x = here_x + dx
        to_y = here_y + dy
        inside.append((to_x >= 0) & (to_x < count_x) & (to_y >= 0) & (to_y < count_y))
        targets.append((lax.rem(to_x + count_x, count_x), lax.rem(to_y + count_y, count_y)))
    barrier = pltpu.get_barrier_semaphore()
    for d in range(9):
        if d != OWN:
            pl.semaphore_signal(
                barrier, inc=1, device_id=targets[d], device_id_type=pl.DeviceIdType.MESH
            )

    for par in range(2):
        land[par, ZERO] = jnp.zeros(land.shape[2:], BF16)

    small[0].wait()
    pattern = pattern_v[...].reshape(bricks, 26)
    lane = lax.broadcasted_iota(jnp.int32, (bricks, 26), 1)
    wide = lax.broadcasted_iota(jnp.int32, (bricks, 128), 1)
    inverse = jnp.zeros((bricks, 128), jnp.int32)
    for t in range(26):
        at = jnp.max(jnp.where(pattern == t, lane, 0), axis=1, keepdims=True)
        inverse = jnp.where(wide == t, at, inverse)
    inverse_v[...] = jnp.zeros(inverse_v.shape, jnp.int32)
    inverse_v[0:bricks] = inverse
    inverse_copy = pltpu.make_async_copy(inverse_v, inverse_s, inverse_sem)
    inverse_copy.start()

    small[1].wait()
    small[2].wait()
    entry = list_v[...]
    live = entry >= 0
    brick = entry >> 3
    octant = jnp.where(live, entry & 7, -1)
    line = (brick * 43691) >> 19
    pos_z = brick - line * bricks
    step_x = (line >> 4) - here_x
    step_y = (line & 15) - here_y
    dest = ((step_x + 1) * 3 + step_y + 1) * bricks + pos_z
    dest = jnp.where(live, dest, -8)

    node = lax.broadcasted_iota(jnp.int32, (values // 3, slots), 0)
    word = jnp.where(
        node < 30, bits_v[0:1, :], jnp.where(node < 60, bits_v[1:2, :], bits_v[2:3, :])
    )
    shift = node - jnp.where(node >= 30, 30, 0) - jnp.where(node >= 60, 30, 0)
    flags = (lax.shift_right_logical(word, shift) & 1).astype(F32)
    flags = jnp.where(live, flags, 0.0)
    mask = jnp.concatenate([flags, flags, flags], axis=0)

    small[3].wait()
    masked = jnp.concatenate(
        [(residual_v[l] * mask).astype(BF16) for l in range(loads)], axis=1
    )
    small[4].wait()
    octants = jnp.concatenate([octant] * loads, axis=1)
    restricted = jnp.zeros((values, loads * slots), F32)
    for o in range(8):
        matrix = restrict_v[o].astype(BF16)
        restrict_b[o] = matrix
        chosen = masked * jnp.where(octants == o, 1.0, 0.0).astype(BF16)
        restricted += dot(matrix, chosen)
    key = jnp.concatenate([dest * 8 + l for l in range(loads)], axis=1)
    row_id = lax.broadcasted_iota(jnp.int32, (9 * rows, loads * slots), 0)
    summing = jnp.where(row_id == key, 1.0, 0.0).astype(BF16)
    outgoing = dot_nt(summing, restricted.astype(BF16))
    for d in range(9):
        part = outgoing[d * rows : (d + 1) * rows]
        tail = jnp.concatenate([part[:, 128:values], jnp.zeros((rows, 256 - values), F32)], axis=1)
        if d == OWN:
            rhs_own[:, 0:128] = part[:, 0:128]
            rhs_own[:, 128:256] = tail
        else:
            rhs_send[SLOT[d], :, 0:128] = part[:, 0:128].astype(BF16)
            rhs_send[SLOT[d], :, 128:256] = tail.astype(BF16)
    pl.semaphore_wait(barrier, 8)
    for d in range(9):
        if d != OWN:
            pltpu.make_async_remote_copy(
                src_ref=rhs_send.at[SLOT[d]],
                dst_ref=rhs_land.at[SLOT[8 - d]],
                send_sem=rhs_sems.at[0],
                recv_sem=rhs_sems.at[1],
                device_id=targets[d],
                device_id_type=pl.DeviceIdType.MESH,
            ).start()

    inverse_copy.wait()
    small[5].wait()

    def block_of(c, d, dz):
        t = d * 3 + dz + 1
        if t == 13:
            return own_v.at[c]
        return raw[c].at[inverse_s[c, t - (1 if t > 13 else 0)]]

    def repack(c):
        big[c].wait()
        partner = 1 if c % 2 == 0 else -1
        edge = c == 0 or c == bricks - 1
        at = 0
        for d in range(9):
            here = block_of(c, d, 0)
            beside = block_of(c, d, partner)
            packed[c, :, at * 128 : (at + 1) * 128] = here[:, 0:128]
            packed[c, :, (at + 1) * 128 : (at + 2) * 128] = beside[:, 0:128]
            packed[c, :, (at + 2) * 128 : (at + 3) * 128] = jnp.concatenate(
                [here[:, 128:values], beside[:, 128:values]], axis=1
            )
            at += 3
            if not edge:
                packed[c, :, at * 128 : (at + 1) * 128] = block_of(c, d, -partner)[:, 0:128]
                at += 1
        if not edge:
            for d, e in JOINED:
                packed[c, :, at * 128 : (at + 1) * 128] = jnp.concatenate(
                    [
                        block_of(c, d, -partner)[:, 128:values],
                        block_of(c, e, -partner)[:, 128:values],
                    ],
                    axis=1,
                )
                at += 1
            last = block_of(c, OWN, -partner)[:, 128:values]
            packed[c, :, at * 128 : (at + 1) * 128] = jnp.concatenate(
                [last, jnp.zeros_like(last)], axis=1
            )

    for c in range(4):
        repack(c)

    square = lax.broadcasted_iota(jnp.int32, (slots, slots), 0) == lax.broadcasted_iota(
        jnp.int32, (slots, slots), 1
    )

    def upright(row):
        return jnp.sum(
            jnp.where(square, row.astype(F32), 0.0), axis=1, keepdims=True
        ).astype(jnp.int32)

    dest_up = upright(dest)
    column_id = lax.broadcasted_iota(jnp.int32, (slots, 9 * rows), 1)
    for l in range(loads):
        gather_v[l * slots : (l + 1) * slots, :] = jnp.where(
            column_id == dest_up * 8 + l, 1.0, 0.0
        ).astype(BF16)
    diagonal = lax.broadcasted_iota(jnp.int32, (values, values), 0) == lax.broadcasted_iota(
        jnp.int32, (values, values), 1
    )
    unit = jnp.where(diagonal, 1.0, 0.0).astype(BF16)
    for o in range(8):
        restrict_t[o] = dot_nt(unit, restrict_b[o]).astype(BF16)

    for p in range(pairs):
        halves = []
        for c in (2 * p, 2 * p + 1):
            found = jnp.sum(
                jnp.where(diagonal, own_v[c].astype(F32), 0.0), axis=0, keepdims=True
            )
            halves.append(jnp.broadcast_to(DAMPING / found, (8, values)))
        scale = jnp.concatenate(halves, axis=0)
        scale_v[p, :, 0:128] = scale[:, 0:128]
        scale_v[p, :, 128:256] = jnp.concatenate(
            [scale[:, 128:values], jnp.zeros((16, 256 - values), F32)], axis=1
        )

    low = lax.broadcasted_iota(jnp.int32, (16, 128), 1) < 64

    def publish(par, p, value):
        tail = value[:, 128:256]
        land[par, SLOT[OWN], p, 0] = value[:, 0:128].astype(BF16)
        land[par, SLOT[OWN], p, 1] = jnp.where(
            low, tail, pltpu.roll(swapped(tail), 64, 1)
        ).astype(BF16)

    def send(par, q):
        for d in range(9):
            if d != OWN:
                source = jnp.where(inside[d], SLOT[OWN], ZERO)
                pltpu.make_async_remote_copy(
                    src_ref=land.at[par, source, pl.ds(2 * q, 2)],
                    dst_ref=land.at[par, SLOT[8 - d], pl.ds(2 * q, 2)],
                    send_sem=send_sems.at[par, q],
                    recv_sem=recv_sems.at[par, q],
                    device_id=targets[d],
                    device_id_type=pl.DeviceIdType.MESH,
                ).start()

    def wait_chunk(par, q, sems):
        part = land.at[par, pl.ds(0, 8), pl.ds(2 * q, 2)]
        pltpu.make_async_copy(part, part, sems.at[par, q]).wait()

    pltpu.make_async_copy(rhs_land, rhs_land, rhs_sems.at[1]).wait()
    for p in range(pairs):
        rhs = rhs_own[16 * p : 16 * p + 16, :]
        for s in range(8):
            rhs += rhs_land[s, 16 * p : 16 * p + 16, :].astype(F32)
        rhs_v[p] = rhs
        first = scale_v[p] * rhs
        solution_v[p] = first
        publish(0, p, first)
    for q in range(3):
        send(0, q)
    pltpu.make_async_copy(rhs_send, rhs_send, rhs_sems.at[0]).wait()

    for c in range(4, bricks):
        repack(c)

    def expand(par, q):
        for p in (2 * q, 2 * q + 1):
            for d in range(9):
                turned[d, p] = swapped(land[par, SLOT[d], p, 0].astype(F32)).astype(BF16)
            for i, (d, e) in enumerate(JOINED + ((OWN, OWN),)):
                left = land[par, SLOT[d], p, 1].astype(F32)
                right = land[par, SLOT[e], p, 1].astype(F32)
                joined[i, p] = jnp.where(low, pltpu.roll(left, 64, 1), right).astype(BF16)

    def apply(par, c):
        p = c // 2
        other = p - 1 if c % 2 == 0 else p + 1
        edge = c == 0 or c == bricks - 1
        tiles = []
        for d in range(9):
            tiles += [land[par, SLOT[d], p, 0], turned[d, p], land[par, SLOT[d], p, 1]]
            if not edge:
                tiles.append(turned[d, other])
        if not edge:
            tiles += [joined[i, other] for i in range(5)]
        depth = 128 * len(tiles)
        return dot_nt(jnp.concatenate(tiles, axis=1), packed[c, :, 0:depth])

    def step(e, carry):
        now = lax.rem(e, 2)
        later = 1 - now

        def finish(p, even, odd):
            applied = jnp.concatenate([even[0:8], odd[8:16]], axis=0)
            applied = jnp.concatenate([applied, jnp.zeros((16, 256 - values), F32)], axis=1)
            value = solution_v[p] + scale_v[p] * (rhs_v[p] - applied)
            solution_v[p] = value
            publish(later, p, value)

        for q in range(3):
            for c in range(4 * q, 4 * q + 4):
                if c == 0:
                    wait_chunk(now, 0, recv_sems)
                    expand(now, 0)
                if c % 4 == 3 and q < 2:
                    wait_chunk(now, q + 1, recv_sems)
                    expand(now, q + 1)
                result = apply(now, c)
                if c % 2 == 0:
                    even = result
                else:
                    finish(c // 2, even, result)
            send(later, q)
            wait_chunk(now, q, send_sems)
        return carry

    lax.fori_loop(0, SWEEPS - 1, step, 0)

    end = (SWEEPS - 1) % 2
    for p in range(pairs):
        for half in range(2):
            coarse_ref[2 * p + half] = solution_v[p, 8 * half : 8 * half + loads, 0:values]
    for q in range(3):
        wait_chunk(end, q, recv_sems)
        wait_chunk(end, q, send_sems)
    around = jnp.concatenate(
        [
            jnp.concatenate([land[end, SLOT[d], p, 0], land[end, SLOT[d], p, 1]], axis=1)
            for d in range(9)
            for p in range(pairs)
        ],
        axis=0,
    )
    fetched = dot(gather_v[...], around)[:, 0:values].astype(BF16)
    octant_up = jnp.concatenate([upright(octant)] * loads, axis=0)
    total = jnp.zeros((values, loads * slots), F32)
    for o in range(8):
        chosen = fetched * jnp.where(octant_up == o, 1.0, 0.0).astype(BF16)
        total += dot_nt(restrict_t[o], chosen)
    for l in range(loads):
        correction_ref[l] = total[:, l * slots : (l + 1) * slots] * mask


def local(fine_list, fine_residual, solid_bits, restrict_ops, operator, pattern):
    slots, loads, values = fine_residual.shape
    bricks = operator.shape[2]
    pairs = bricks // 2
    rows = bricks * 8
    any_space = pl.BlockSpec(memory_space=pl.ANY)
    vmem = pl.BlockSpec(memory_space=pltpu.VMEM)
    dma = pltpu.SemaphoreType.DMA
    correction, coarse = pl.pallas_call(
        kernel,
        out_shape=[
            jax.ShapeDtypeStruct((loads, values, slots), F32),
            jax.ShapeDtypeStruct((bricks, loads, values), F32),
        ],
        in_specs=[any_space] * 6,
        out_specs=[vmem, vmem],
        scratch_shapes=[
            pltpu.VMEM((1, slots), jnp.int32),
            pltpu.VMEM((3, slots), jnp.int32),
            pltpu.VMEM((loads, values, slots), F32),
            pltpu.VMEM((8, values, values), F32),
            pltpu.VMEM((bricks, values, values), BF16),
            pltpu.VMEM((bricks, 1, 26), jnp.int32),
            pltpu.VMEM((16, 128), jnp.int32),
            pltpu.SMEM((16, 128), jnp.int32),
            pltpu.VMEM((bricks, values, 41 * 128), BF16),
            pltpu.VMEM((8, values, values), BF16),
            pltpu.VMEM((8, values, values), BF16),
            pltpu.VMEM((loads * slots, 9 * rows), BF16),
            pltpu.VMEM((rows, 256), F32),
            pltpu.VMEM((8, rows, 256), BF16),
            pltpu.VMEM((8, rows, 256), BF16),
            pltpu.VMEM((2, 10, pairs, 2, 16, 128), BF16),
            pltpu.VMEM((9, pairs, 16, 128), BF16),
            pltpu.VMEM((5, pairs, 16, 128), BF16),
            pltpu.VMEM((pairs, 16, 256), F32),
            pltpu.VMEM((pairs, 16, 256), F32),
            pltpu.VMEM((pairs, 16, 256), F32),
            dma((6,)),
            dma((bricks,)),
            dma,
            dma((2,)),
            dma((2, 3)),
            dma((2, 3)),
        ]
        + [pltpu.VMEM((26, values, values), BF16)] * bricks,
        compiler_params=pltpu.CompilerParams(
            collective_id=0, has_side_effects=True, vmem_limit_bytes=63 * 2**20
        ),
    )(
        fine_list.reshape(1, slots),
        solid_bits.T,
        fine_residual.transpose(1, 2, 0),
        restrict_ops,
        operator.reshape(bricks, 27, values, values),
        pattern.reshape(bricks, 1, 26),
    )
    return correction.transpose(2, 0, 1), coarse.reshape(1, 1, bricks, loads, values)


def solution(mesh):
    in_specs = (
        P(("gx", "gy")),
        P(("gx", "gy"), None, None),
        P(("gx", "gy"), None),
        P(),
        P("gx", "gy", None, None, None, None),
        P("gx", "gy", None, None),
    )
    out_specs = (P(("gx", "gy"), None, None), P("gx", "gy", None, None, None))
    return jax.shard_map(local, mesh=mesh, in_specs=in_specs, out_specs=out_specs, check_vma=False)
```

time: 314 us -> 111 us (0.35)
  the two profiles are of different devices: /device:TPU:105 before, /device:TPU:1 now
where the time goes in v1:
time: 111 us
  Pallas kernels  107 us (96%)
  local copies, waits for them, and re-layouts  3.52 us (3%)
    pallas_call x1, Pallas kernels, local(): pl.pallas_call(kernel, out_shape=[jax.ShapeDtypeStruct((loads, values, sl...  107 us
    unnamed x2, local copies, waits for them, and re-layouts  3.52 us

profile of v1, /device:TPU:1, one launch (start us, length us, event | category | flops | bytes accessed | tf_op | source)
XLA Modules:
  0.0 110.7 jit_solution(10706943615285646666)
XLA Ops:
  0.6 106.6 %shard_map.77 = (f32[6,192,128]{2,1,0:T(8,128)}, f32[12,6,192]{2,1,0:T(8,128)}) custom-call(s32[1,128]{1,0:T(1,128)} %bitcast.13, s32[3,128]{1,0:T(4,128)} %bitcast.12, f32[6,192,128]{2,1,0:T(8,128)} %bitcast.9, f32[8,192,192]{2,1,0:T(8,128)} %restrict_hbm.1, bf16[12,27,192,192]{3,2,1,0:T(8,128)(2,1)} %bitcast.7, s32[12,1,26]{2,1,0:T(1,128)} %bitcast.11), custom_call_target="tpu_custom_call" | custom-call | tf_op jit(solution)/shard_map/pallas_call | solution.py:372
  107.2 1.6 %copy.8 = f32[1,1,12,6,192]{4,1,3,2,0:T(1,128)} copy(f32[1,1,12,6,192]{4,3,2,1,0:T(8,128)} %bitcast.10) | data formatting | bytes 110592
  108.8 1.9 %copy.10 = f32[128,6,192]{0,2,1:T(8,128)} copy(f32[128,6,192]{0,2,1:T(8,128)} %bitcast.8) | data formatting | bytes 1179648

commit v2 on v1

--- a/solution.py
+++ b/solution.py
@@ -10,9 +10,8 @@
 DAMPING = 0.8
 OFFSETS = [(dx, dy) for dx in (-1, 0, 1) for dy in (-1, 0, 1)]
 OWN = 4
+AHEAD = 4
 SLOT = {d: (d if d < OWN else d - 1) for d in range(9) if d != OWN}
-SLOT[OWN] = 8
-ZERO = 9
 JOINED = ((0, 1), (2, 3), (5, 6), (7, 8))
 NT = (((1,), (1,)), ((), ()))
 F32 = jnp.float32
@@ -36,7 +35,7 @@
     correction_ref, coarse_ref,
     list_v, bits_v, residual_v, restrict_v, own_v, pattern_v, inverse_v, inverse_s,
     packed, restrict_b, restrict_t, gather_v, rhs_own, rhs_send, rhs_land,
-    land, turned, joined, solution_v, rhs_v, scale_v,
+    land, own, turned, joined, solution_v, rhs_v, scale_v,
     small_sem, raw_sem, inverse_sem, rhs_sems, send_sems, recv_sems,
     *raw,
 ):
@@ -70,25 +69,42 @@
         pltpu.make_async_copy(operator_hbm.at[c, pl.ds(1, 26)], raw[c], raw_sem.at[c])
         for c in range(bricks)
     ]
-    for copy in big:
-        copy.start()
-
-    targets = []
-    inside = []
+
+    land[...] = jnp.zeros(land.shape, BF16)
+    rhs_land[...] = jnp.zeros(rhs_land.shape, BF16)
+
+    inside = {}
+    around_x = 3 - (here_x == 0).astype(jnp.int32) - (here_x == count_x - 1).astype(jnp.int32)
+    around_y = 3 - (here_y == 0).astype(jnp.int32) - (here_y == count_y - 1).astype(jnp.int32)
+    beside = around_x * around_y - 1
     for d, (dx, dy) in enumerate(OFFSETS):
         to_x = here_x + dx
         to_y = here_y + dy
-        inside.append((to_x >= 0) & (to_x < count_x) & (to_y >= 0) & (to_y < count_y))
-        targets.append((lax.rem(to_x + count_x, count_x), lax.rem(to_y + count_y, count_y)))
+        if d != OWN:
+            inside[d] = (to_x >= 0) & (to_x < count_x) & (to_y >= 0) & (to_y < count_y)
+
+    def to_each(action):
+        for d, (dx, dy) in enumerate(OFFSETS):
+            if d != OWN:
+
+                @pl.when(inside[d])
+                def _():
+                    action(d, (here_x + dx, here_y + dy))
+
+    def wait_each(part, sem):
+        for count in (8, 5, 3):
+
+            @pl.when(beside == count)
+            def _():
+                some = part.at[pl.ds(0, count)]
+                pltpu.make_async_copy(some, some, sem).wait()
+
     barrier = pltpu.get_barrier_semaphore()
-    for d in range(9):
-        if d != OWN:
-            pl.semaphore_signal(
-                barrier, inc=1, device_id=targets[d], device_id_type=pl.DeviceIdType.MESH
-            )
-
-    for par in range(2):
-        land[par, ZERO] = jnp.zeros(land.shape[2:], BF16)
+    to_each(
+        lambda d, target: pl.semaphore_signal(
+            barrier, inc=1, device_id=target, device_id_type=pl.DeviceIdType.MESH
+        )
+    )
 
     small[0].wait()
     pattern = pattern_v[...].reshape(bricks, 26)
@@ -130,6 +146,8 @@
         [(residual_v[l] * mask).astype(BF16) for l in range(loads)], axis=1
     )
     small[4].wait()
+    for c in range(AHEAD):
+        big[c].start()
     octants = jnp.concatenate([octant] * loads, axis=1)
     restricted = jnp.zeros((values, loads * slots), F32)
     for o in range(8):
@@ -141,26 +159,17 @@
     row_id = lax.broadcasted_iota(jnp.int32, (9 * rows, loads * slots), 0)
     summing = jnp.where(row_id == key, 1.0, 0.0).astype(BF16)
     outgoing = dot_nt(summing, restricted.astype(BF16))
+    low_half = lax.broadcasted_iota(jnp.int32, (rows // 2, 128), 1) < 64
     for d in range(9):
         part = outgoing[d * rows : (d + 1) * rows]
         tail = jnp.concatenate([part[:, 128:values], jnp.zeros((rows, 256 - values), F32)], axis=1)
+        tail = jnp.where(low_half, tail[: rows // 2], pltpu.roll(tail[rows // 2 :], 64, 1))
         if d == OWN:
-            rhs_own[:, 0:128] = part[:, 0:128]
-            rhs_own[:, 128:256] = tail
+            rhs_own[0:rows] = part[:, 0:128]
+            rhs_own[rows:] = tail
         else:
-            rhs_send[SLOT[d], :, 0:128] = part[:, 0:128].astype(BF16)
-            rhs_send[SLOT[d], :, 128:256] = tail.astype(BF16)
-    pl.semaphore_wait(barrier, 8)
-    for d in range(9):
-        if d != OWN:
-            pltpu.make_async_remote_copy(
-                src_ref=rhs_send.at[SLOT[d]],
-                dst_ref=rhs_land.at[SLOT[8 - d]],
-                send_sem=rhs_sems.at[0],
-                recv_sem=rhs_sems.at[1],
-                device_id=targets[d],
-                device_id_type=pl.DeviceIdType.MESH,
-            ).start()
+            rhs_send[SLOT[d], 0:rows] = part[:, 0:128].astype(BF16)
+            rhs_send[SLOT[d], rows:] = tail.astype(BF16)
 
     inverse_copy.wait()
     small[5].wait()
@@ -173,21 +182,21 @@
 
     def repack(c):
         big[c].wait()
+        if c + AHEAD < bricks:
+            big[c + AHEAD].start()
         partner = 1 if c % 2 == 0 else -1
         edge = c == 0 or c == bricks - 1
-        at = 0
         for d in range(9):
             here = block_of(c, d, 0)
-            beside = block_of(c, d, partner)
-            packed[c, :, at * 128 : (at + 1) * 128] = here[:, 0:128]
-            packed[c, :, (at + 1) * 128 : (at + 2) * 128] = beside[:, 0:128]
-            packed[c, :, (at + 2) * 128 : (at + 3) * 128] = jnp.concatenate(
-                [here[:, 128:values], beside[:, 128:values]], axis=1
+            near = block_of(c, d, partner)
+            packed[c, :, d * 128 : (d + 1) * 128] = here[:, 0:128]
+            packed[c, :, (9 + d) * 128 : (10 + d) * 128] = jnp.concatenate(
+                [here[:, 128:values], near[:, 128:values]], axis=1
             )
-            at += 3
+            packed[c, :, (18 + d) * 128 : (19 + d) * 128] = near[:, 0:128]
             if not edge:
-                packed[c, :, at * 128 : (at + 1) * 128] = block_of(c, d, -partner)[:, 0:128]
-                at += 1
+                packed[c, :, (27 + d) * 128 : (28 + d) * 128] = block_of(c, d, -partner)[:, 0:128]
+        at = 36
         if not edge:
             for d, e in JOINED:
                 packed[c, :, at * 128 : (at + 1) * 128] = jnp.concatenate(
@@ -203,7 +212,22 @@
                 [last, jnp.zeros_like(last)], axis=1
             )
 
-    for c in range(4):
+    for c in range(3):
+        repack(c)
+
+    pl.semaphore_wait(barrier, beside)
+    to_each(
+        lambda d, target: pltpu.make_async_remote_copy(
+            src_ref=rhs_send.at[SLOT[d]],
+            dst_ref=rhs_land.at[SLOT[8 - d]],
+            send_sem=rhs_sems.at[0],
+            recv_sem=rhs_sems.at[1],
+            device_id=target,
+            device_id_type=pl.DeviceIdType.MESH,
+        ).start()
+    )
+
+    for c in range(3, 7):
         repack(c)
 
     square = lax.broadcasted_iota(jnp.int32, (slots, slots), 0) == lax.broadcasted_iota(
@@ -245,63 +269,69 @@
 
     def publish(par, p, value):
         tail = value[:, 128:256]
-        land[par, SLOT[OWN], p, 0] = value[:, 0:128].astype(BF16)
-        land[par, SLOT[OWN], p, 1] = jnp.where(
-            low, tail, pltpu.roll(swapped(tail), 64, 1)
-        ).astype(BF16)
+        own[par, p, 0] = value[:, 0:128].astype(BF16)
+        own[par, p, 1] = jnp.where(low, tail, pltpu.roll(swapped(tail), 64, 1)).astype(BF16)
 
     def send(par, q):
-        for d in range(9):
-            if d != OWN:
-                source = jnp.where(inside[d], SLOT[OWN], ZERO)
-                pltpu.make_async_remote_copy(
-                    src_ref=land.at[par, source, pl.ds(2 * q, 2)],
-                    dst_ref=land.at[par, SLOT[8 - d], pl.ds(2 * q, 2)],
-                    send_sem=send_sems.at[par, q],
-                    recv_sem=recv_sems.at[par, q],
-                    device_id=targets[d],
-                    device_id_type=pl.DeviceIdType.MESH,
-                ).start()
+        to_each(
+            lambda d, target: pltpu.make_async_remote_copy(
+                src_ref=own.at[par, pl.ds(2 * q, 2)],
+                dst_ref=land.at[par, SLOT[8 - d], pl.ds(2 * q, 2)],
+                send_sem=send_sems.at[par, q],
+                recv_sem=recv_sems.at[par, q],
+                device_id=target,
+                device_id_type=pl.DeviceIdType.MESH,
+            ).start()
+        )
 
     def wait_chunk(par, q, sems):
-        part = land.at[par, pl.ds(0, 8), pl.ds(2 * q, 2)]
-        pltpu.make_async_copy(part, part, sems.at[par, q]).wait()
-
-    pltpu.make_async_copy(rhs_land, rhs_land, rhs_sems.at[1]).wait()
+        wait_each(land.at[par, :, pl.ds(2 * q, 2)], sems.at[par, q])
+
+    def column(par, d, p, kind):
+        return own[par, p, kind] if d == OWN else land[par, SLOT[d], p, kind]
+
+    wait_each(rhs_land, rhs_sems.at[1])
     for p in range(pairs):
-        rhs = rhs_own[16 * p : 16 * p + 16, :]
-        for s in range(8):
-            rhs += rhs_land[s, 16 * p : 16 * p + 16, :].astype(F32)
+        def rhs_rows(r):
+            total = rhs_own[r : r + 16]
+            for s in range(8):
+                total += rhs_land[s, r : r + 16].astype(F32)
+            return total
+
+        head = rhs_rows(16 * p)
+        tail = rhs_rows(rows + 16 * (p % (pairs // 2)))
+        if p >= pairs // 2:
+            tail = pltpu.roll(tail, 64, 1)
+        rhs = jnp.concatenate([head, tail], axis=1)
         rhs_v[p] = rhs
         first = scale_v[p] * rhs
         solution_v[p] = first
         publish(0, p, first)
-    for q in range(3):
-        send(0, q)
-    pltpu.make_async_copy(rhs_send, rhs_send, rhs_sems.at[0]).wait()
-
-    for c in range(4, bricks):
+        if p % 2 == 1:
+            send(0, p // 2)
+    wait_each(rhs_send, rhs_sems.at[0])
+
+    for c in range(7, bricks):
         repack(c)
 
     def expand(par, q):
         for p in (2 * q, 2 * q + 1):
             for d in range(9):
-                turned[d, p] = swapped(land[par, SLOT[d], p, 0].astype(F32)).astype(BF16)
+                turned[d, p] = swapped(column(par, d, p, 0).astype(F32)).astype(BF16)
             for i, (d, e) in enumerate(JOINED + ((OWN, OWN),)):
-                left = land[par, SLOT[d], p, 1].astype(F32)
-                right = land[par, SLOT[e], p, 1].astype(F32)
+                left = column(par, d, p, 1).astype(F32)
+                right = column(par, e, p, 1).astype(F32)
                 joined[i, p] = jnp.where(low, pltpu.roll(left, 64, 1), right).astype(BF16)
 
     def apply(par, c):
         p = c // 2
         other = p - 1 if c % 2 == 0 else p + 1
         edge = c == 0 or c == bricks - 1
-        tiles = []
-        for d in range(9):
-            tiles += [land[par, SLOT[d], p, 0], turned[d, p], land[par, SLOT[d], p, 1]]
-            if not edge:
-                tiles.append(turned[d, other])
+        tiles = [column(par, d, p, 0) for d in range(9)]
+        tiles += [column(par, d, p, 1) for d in range(9)]
+        tiles += [turned[d, p] for d in range(9)]
         if not edge:
+            tiles += [turned[d, other] for d in range(9)]
             tiles += [joined[i, other] for i in range(5)]
         depth = 128 * len(tiles)
         return dot_nt(jnp.concatenate(tiles, axis=1), packed[c, :, 0:depth])
@@ -345,7 +375,7 @@
         wait_chunk(end, q, send_sems)
     around = jnp.concatenate(
         [
-            jnp.concatenate([land[end, SLOT[d], p, 0], land[end, SLOT[d], p, 1]], axis=1)
+            jnp.concatenate([column(end, d, p, 0), column(end, d, p, 1)], axis=1)
             for d in range(9)
             for p in range(pairs)
         ],
@@ -390,10 +420,11 @@
             pltpu.VMEM((8, values, values), BF16),
             pltpu.VMEM((8, values, values), BF16),
             pltpu.VMEM((loads * slots, 9 * rows), BF16),
-            pltpu.VMEM((rows, 256), F32),
-            pltpu.VMEM((8, rows, 256), BF16),
-            pltpu.VMEM((8, rows, 256), BF16),
-            pltpu.VMEM((2, 10, pairs, 2, 16, 128), BF16),
+            pltpu.VMEM((rows * 3 // 2, 128), F32),
+            pltpu.VMEM((8, rows * 3 // 2, 128), BF16),
+            pltpu.VMEM((8, rows * 3 // 2, 128), BF16),
+            pltpu.VMEM((2, 8, pairs, 2, 16, 128), BF16),
+            pltpu.VMEM((2, pairs, 2, 16, 128), BF16),
             pltpu.VMEM((9, pairs, 16, 128), BF16),
             pltpu.VMEM((5, pairs, 16, 128), BF16),
             pltpu.VMEM((pairs, 16, 256), F32),

time: 111 us -> 91.6 us (0.83)
  the two profiles are of different devices: /device:TPU:1 before, /device:TPU:105 now
where the time goes in v2:
time: 91.6 us; the launch traced here: 91.4 us
  Pallas kernels  87.2 us (95%)
  local copies, waits for them, and re-layouts  3.52 us (4%)
    pallas_call x1, Pallas kernels, local(): pl.pallas_call(kernel, out_shape=[jax.ShapeDtypeStruct((loads, values, sl...  87.2 us
    unnamed x2, local copies, waits for them, and re-layouts  3.52 us

profile of v2, /device:TPU:105, one launch (start us, length us, event | category | flops | bytes accessed | tf_op | source)
XLA Modules:
  0.0 91.4 jit_solution(545421461458445628)
XLA Ops:
  0.6 87.2 %shard_map.77 = (f32[6,192,128]{2,1,0:T(8,128)}, f32[12,6,192]{2,1,0:T(8,128)}) custom-call(s32[1,128]{1,0:T(1,128)} %bitcast.13, s32[3,128]{1,0:T(4,128)} %bitcast.12, f32[6,192,128]{2,1,0:T(8,128)} %bitcast.9, f32[8,192,192]{2,1,0:T(8,128)} %restrict_hbm.1, bf16[12,27,192,192]{3,2,1,0:T(8,128)(2,1)} %bitcast.7, s32[12,1,26]{2,1,0:T(1,128)} %bitcast.11), custom_call_target="tpu_custom_call" | custom-call | tf_op jit(solution)/shard_map/pallas_call | solution.py:402
  87.9 1.6 %copy.8 = f32[1,1,12,6,192]{4,1,3,2,0:T(1,128)} copy(f32[1,1,12,6,192]{4,3,2,1,0:T(8,128)} %bitcast.10) | data formatting | bytes 110592
  89.5 1.9 %copy.10 = f32[128,6,192]{0,2,1:T(8,128)} copy(f32[128,6,192]{0,2,1:T(8,128)} %bitcast.8) | data formatting | bytes 1179648

commit v3 on v2

--- a/solution.py
+++ b/solution.py
@@ -10,6 +10,9 @@
 DAMPING = 0.8
 OFFSETS = [(dx, dy) for dx in (-1, 0, 1) for dy in (-1, 0, 1)]
 OWN = 4
+NEIGHBOURS = [d for d in range(9) if d != OWN]
+ARRIVE = (0, 3, 7)
+LEAVE = (3, 7, 11)
 AHEAD = 4
 SLOT = {d: (d if d < OWN else d - 1) for d in range(9) if d != OWN}
 JOINED = ((0, 1), (2, 3), (5, 6), (7, 8))
@@ -35,7 +38,7 @@
     correction_ref, coarse_ref,
     list_v, bits_v, residual_v, restrict_v, own_v, pattern_v, inverse_v, inverse_s,
     packed, restrict_b, restrict_t, gather_v, rhs_own, rhs_send, rhs_land,
-    land, own, turned, joined, solution_v, rhs_v, scale_v,
+    land, own, turned, joined, applied_v, solution_v, rhs_v, scale_v,
     small_sem, raw_sem, inverse_sem, rhs_sems, send_sems, recv_sems,
     *raw,
 ):
@@ -73,6 +76,8 @@
     land[...] = jnp.zeros(land.shape, BF16)
     rhs_land[...] = jnp.zeros(rhs_land.shape, BF16)
 
+    applied_v[...] = jnp.zeros(applied_v.shape, F32)
+
     inside = {}
     around_x = 3 - (here_x == 0).astype(jnp.int32) - (here_x == count_x - 1).astype(jnp.int32)
     around_y = 3 - (here_y == 0).astype(jnp.int32) - (here_y == count_y - 1).astype(jnp.int32)
@@ -84,12 +89,12 @@
             inside[d] = (to_x >= 0) & (to_x < count_x) & (to_y >= 0) & (to_y < count_y)
 
     def to_each(action):
-        for d, (dx, dy) in enumerate(OFFSETS):
-            if d != OWN:
-
-                @pl.when(inside[d])
-                def _():
-                    action(d, (here_x + dx, here_y + dy))
+        for d in (0, 2, 6, 8, 3, 5, 1, 7):
+            dx, dy = OFFSETS[d]
+
+            @pl.when(inside[d])
+            def _():
+                action(d, (here_x + dx, here_y + dy))
 
     def wait_each(part, sem):
         for count in (8, 5, 3):
@@ -186,31 +191,37 @@
             big[c + AHEAD].start()
         partner = 1 if c % 2 == 0 else -1
         edge = c == 0 or c == bricks - 1
-        for d in range(9):
+
+        def put(at, value):
+            packed[c, :, at * 128 : (at + 1) * 128] = value
+
+        def halves(left, right):
+            return jnp.concatenate([left[:, 128:values], right[:, 128:values]], axis=1)
+
+        at = 0
+        here = block_of(c, OWN, 0)
+        near = block_of(c, OWN, partner)
+        put(0, here[:, 0:128])
+        put(1, halves(here, near))
+        put(2, near[:, 0:128])
+        at = 3
+        if not edge:
+            far = block_of(c, OWN, -partner)
+            put(3, far[:, 0:128])
+            last = far[:, 128:values]
+            put(4, jnp.concatenate([last, jnp.zeros_like(last)], axis=1))
+            at = 5
+        for i, d in enumerate(NEIGHBOURS):
             here = block_of(c, d, 0)
             near = block_of(c, d, partner)
-            packed[c, :, d * 128 : (d + 1) * 128] = here[:, 0:128]
-            packed[c, :, (9 + d) * 128 : (10 + d) * 128] = jnp.concatenate(
-                [here[:, 128:values], near[:, 128:values]], axis=1
-            )
-            packed[c, :, (18 + d) * 128 : (19 + d) * 128] = near[:, 0:128]
+            put(at + i, here[:, 0:128])
+            put(at + 8 + i, halves(here, near))
+            put(at + 16 + i, near[:, 0:128])
             if not edge:
-                packed[c, :, (27 + d) * 128 : (28 + d) * 128] = block_of(c, d, -partner)[:, 0:128]
-        at = 36
+                put(at + 24 + i, block_of(c, d, -partner)[:, 0:128])
         if not edge:
-            for d, e in JOINED:
-                packed[c, :, at * 128 : (at + 1) * 128] = jnp.concatenate(
-                    [
-                        block_of(c, d, -partner)[:, 128:values],
-                        block_of(c, e, -partner)[:, 128:values],
-                    ],
-                    axis=1,
-                )
-                at += 1
-            last = block_of(c, OWN, -partner)[:, 128:values]
-            packed[c, :, at * 128 : (at + 1) * 128] = jnp.concatenate(
-                [last, jnp.zeros_like(last)], axis=1
-            )
+            for i, (d, e) in enumerate(JOINED):
+                put(at + 32 + i, halves(block_of(c, d, -partner), block_of(c, e, -partner)))
 
     for c in range(3):
         repack(c)
@@ -271,6 +282,8 @@
         tail = value[:, 128:256]
         own[par, p, 0] = value[:, 0:128].astype(BF16)
         own[par, p, 1] = jnp.where(low, tail, pltpu.roll(swapped(tail), 64, 1)).astype(BF16)
+        turned[OWN, p] = swapped(value[:, 0:128]).astype(BF16)
+        joined[len(JOINED), p] = swapped(tail).astype(BF16)
 
     def send(par, q):
         to_each(
@@ -316,52 +329,63 @@
 
     def expand(par, q):
         for p in (2 * q, 2 * q + 1):
-            for d in range(9):
-                turned[d, p] = swapped(column(par, d, p, 0).astype(F32)).astype(BF16)
-            for i, (d, e) in enumerate(JOINED + ((OWN, OWN),)):
-                left = column(par, d, p, 1).astype(F32)
-                right = column(par, e, p, 1).astype(F32)
+            for d in NEIGHBOURS:
+                turned[d, p] = swapped(land[par, SLOT[d], p, 0].astype(F32)).astype(BF16)
+            for i, (d, e) in enumerate(JOINED):
+                left = land[par, SLOT[d], p, 1].astype(F32)
+                right = land[par, SLOT[e], p, 1].astype(F32)
                 joined[i, p] = jnp.where(low, pltpu.roll(left, 64, 1), right).astype(BF16)
 
-    def apply(par, c):
+    def apply(par, c, columns, pairs_joined, at):
         p = c // 2
         other = p - 1 if c % 2 == 0 else p + 1
-        edge = c == 0 or c == bricks - 1
-        tiles = [column(par, d, p, 0) for d in range(9)]
-        tiles += [column(par, d, p, 1) for d in range(9)]
-        tiles += [turned[d, p] for d in range(9)]
-        if not edge:
-            tiles += [turned[d, other] for d in range(9)]
-            tiles += [joined[i, other] for i in range(5)]
+        tiles = [column(par, d, p, 0) for d in columns]
+        tiles += [column(par, d, p, 1) for d in columns]
+        tiles += [turned[d, p] for d in columns]
+        if c != 0 and c != bricks - 1:
+            tiles += [turned[d, other] for d in columns]
+            tiles += [joined[i, other] for i in pairs_joined]
         depth = 128 * len(tiles)
-        return dot_nt(jnp.concatenate(tiles, axis=1), packed[c, :, 0:depth])
+        return dot_nt(jnp.concatenate(tiles, axis=1), packed[c, :, at : at + depth])
+
+    def apply_own(par, c):
+        return apply(par, c, [OWN], [len(JOINED)], 0)
+
+    def apply_neighbours(par, c):
+        at = 3 if c == 0 or c == bricks - 1 else 5
+        return apply(par, c, NEIGHBOURS, range(len(JOINED)), 128 * at)
 
     def step(e, carry):
         now = lax.rem(e, 2)
         later = 1 - now
 
-        def finish(p, even, odd):
-            applied = jnp.concatenate([even[0:8], odd[8:16]], axis=0)
-            applied = jnp.concatenate([applied, jnp.zeros((16, 256 - values), F32)], axis=1)
-            value = solution_v[p] + scale_v[p] * (rhs_v[p] - applied)
+        def keep(c, result, add):
+            part = slice(0, 8) if c % 2 == 0 else slice(8, 16)
+            for lanes in (slice(0, 128), slice(128, values)):
+                kept = result[part, lanes]
+                if add:
+                    kept += applied_v[c // 2, part, lanes]
+                applied_v[c // 2, part, lanes] = kept
+
+        def finish(p):
+            value = solution_v[p] + scale_v[p] * (rhs_v[p] - applied_v[p])
             solution_v[p] = value
             publish(later, p, value)
 
-        for q in range(3):
-            for c in range(4 * q, 4 * q + 4):
-                if c == 0:
-                    wait_chunk(now, 0, recv_sems)
-                    expand(now, 0)
-                if c % 4 == 3 and q < 2:
-                    wait_chunk(now, q + 1, recv_sems)
-                    expand(now, q + 1)
-                result = apply(now, c)
-                if c % 2 == 0:
-                    even = result
-                else:
-                    finish(c // 2, even, result)
-            send(later, q)
-            wait_chunk(now, q, send_sems)
+        for c in range(bricks):
+            keep(c, apply_own(now, c), False)
+        for c in range(bricks):
+            if c in ARRIVE:
+                q = ARRIVE.index(c)
+                wait_chunk(now, q, recv_sems)
+                expand(now, q)
+            keep(c, apply_neighbours(now, c), True)
+            if c % 2 == 1:
+                finish(c // 2)
+            if c in LEAVE:
+                q = LEAVE.index(c)
+                send(later, q)
+                wait_chunk(now, q, send_sems)
         return carry
 
     lax.fori_loop(0, SWEEPS - 1, step, 0)
@@ -430,6 +454,7 @@
             pltpu.VMEM((pairs, 16, 256), F32),
             pltpu.VMEM((pairs, 16, 256), F32),
             pltpu.VMEM((pairs, 16, 256), F32),
+            pltpu.VMEM((pairs, 16, 256), F32),
             dma((6,)),
             dma((bricks,)),
             dma,

time: 91.6 us -> 77.3 us (0.84)
  Pallas kernels: 87.2 us -> 72.8 us
    pallas_call x1, Pallas kernels: 87.2 us -> 72.8 us  [local(): pl.pallas_call(kernel, out_shape=[jax.ShapeDtypeStruct((loads, values, sl...]
where the time goes in v3:
time: 77.3 us; the launch traced here: 76.9 us
  Pallas kernels  72.8 us (94%)
  local copies, waits for them, and re-layouts  3.52 us (5%)
    pallas_call x1, Pallas kernels, local(): pl.pallas_call(kernel, out_shape=[jax.ShapeDtypeStruct((loads, values, sl...  72.8 us
    unnamed x2, local copies, waits for them, and re-layouts  3.52 us

profile of v3, /device:TPU:105, one launch (start us, length us, event | category | flops | bytes accessed | tf_op | source)
XLA Modules:
  0.0 76.9 jit_solution(907192247176432084)
XLA Ops:
  0.6 72.8 %shard_map.77 = (f32[6,192,128]{2,1,0:T(8,128)}, f32[12,6,192]{2,1,0:T(8,128)}) custom-call(s32[1,128]{1,0:T(1,128)} %bitcast.13, s32[3,128]{1,0:T(4,128)} %bitcast.12, f32[6,192,128]{2,1,0:T(8,128)} %bitcast.9, f32[8,192,192]{2,1,0:T(8,128)} %restrict_hbm.1, bf16[12,27,192,192]{3,2,1,0:T(8,128)(2,1)} %bitcast.7, s32[12,1,26]{2,1,0:T(1,128)} %bitcast.11), custom_call_target="tpu_custom_call" | custom-call | tf_op jit(solution)/shard_map/pallas_call | solution.py:426
  73.4 1.6 %copy.8 = f32[1,1,12,6,192]{4,1,3,2,0:T(1,128)} copy(f32[1,1,12,6,192]{4,3,2,1,0:T(8,128)} %bitcast.10) | data formatting | bytes 110592
  75.0 1.9 %copy.10 = f32[128,6,192]{0,2,1:T(8,128)} copy(f32[128,6,192]{0,2,1:T(8,128)} %bitcast.8) | data formatting | bytes 1179648

commit v4 on v3

--- a/solution.py
+++ b/solution.py
@@ -12,7 +12,7 @@
 OWN = 4
 NEIGHBOURS = [d for d in range(9) if d != OWN]
 ARRIVE = (0, 3, 7)
-LEAVE = (3, 7, 11)
+LEAVE = (4, 7, 11)
 AHEAD = 4
 SLOT = {d: (d if d < OWN else d - 1) for d in range(9) if d != OWN}
 JOINED = ((0, 1), (2, 3), (5, 6), (7, 8))
@@ -164,17 +164,19 @@
     row_id = lax.broadcasted_iota(jnp.int32, (9 * rows, loads * slots), 0)
     summing = jnp.where(row_id == key, 1.0, 0.0).astype(BF16)
     outgoing = dot_nt(summing, restricted.astype(BF16))
-    low_half = lax.broadcasted_iota(jnp.int32, (rows // 2, 128), 1) < 64
+    low = lax.broadcasted_iota(jnp.int32, (16, 128), 1) < 64
     for d in range(9):
-        part = outgoing[d * rows : (d + 1) * rows]
-        tail = jnp.concatenate([part[:, 128:values], jnp.zeros((rows, 256 - values), F32)], axis=1)
-        tail = jnp.where(low_half, tail[: rows // 2], pltpu.roll(tail[rows // 2 :], 64, 1))
-        if d == OWN:
-            rhs_own[0:rows] = part[:, 0:128]
-            rhs_own[rows:] = tail
-        else:
-            rhs_send[SLOT[d], 0:rows] = part[:, 0:128].astype(BF16)
-            rhs_send[SLOT[d], rows:] = tail.astype(BF16)
+        for q in range(3):
+            at = d * rows + 32 * q
+            part = outgoing[at : at + 32]
+            tail = jnp.concatenate([part[:, 128:values], jnp.zeros((32, 256 - values), F32)], axis=1)
+            tail = jnp.where(low, tail[0:16], pltpu.roll(tail[16:32], 64, 1))
+            if d == OWN:
+                rhs_own[q, 0:32] = part[:, 0:128]
+                rhs_own[q, 32:48] = tail
+            else:
+                rhs_send[SLOT[d], q, 0:32] = part[:, 0:128].astype(BF16)
+                rhs_send[SLOT[d], q, 32:48] = tail.astype(BF16)
 
     inverse_copy.wait()
     small[5].wait()
@@ -227,16 +229,17 @@
         repack(c)
 
     pl.semaphore_wait(barrier, beside)
-    to_each(
-        lambda d, target: pltpu.make_async_remote_copy(
-            src_ref=rhs_send.at[SLOT[d]],
-            dst_ref=rhs_land.at[SLOT[8 - d]],
-            send_sem=rhs_sems.at[0],
-            recv_sem=rhs_sems.at[1],
-            device_id=target,
-            device_id_type=pl.DeviceIdType.MESH,
-        ).start()
-    )
+    for q in range(3):
+        to_each(
+            lambda d, target, q=q: pltpu.make_async_remote_copy(
+                src_ref=rhs_send.at[SLOT[d], q],
+                dst_ref=rhs_land.at[SLOT[8 - d], q],
+                send_sem=rhs_sems.at[0, q],
+                recv_sem=rhs_sems.at[1, q],
+                device_id=target,
+                device_id_type=pl.DeviceIdType.MESH,
+            ).start()
+        )
 
     for c in range(3, 7):
         repack(c)
@@ -276,8 +279,6 @@
             [scale[:, 128:values], jnp.zeros((16, 256 - values), F32)], axis=1
         )
 
-    low = lax.broadcasted_iota(jnp.int32, (16, 128), 1) < 64
-
     def publish(par, p, value):
         tail = value[:, 128:256]
         own[par, p, 0] = value[:, 0:128].astype(BF16)
@@ -303,26 +304,22 @@
     def column(par, d, p, kind):
         return own[par, p, kind] if d == OWN else land[par, SLOT[d], p, kind]
 
-    wait_each(rhs_land, rhs_sems.at[1])
-    for p in range(pairs):
-        def rhs_rows(r):
-            total = rhs_own[r : r + 16]
-            for s in range(8):
-                total += rhs_land[s, r : r + 16].astype(F32)
-            return total
-
-        head = rhs_rows(16 * p)
-        tail = rhs_rows(rows + 16 * (p % (pairs // 2)))
-        if p >= pairs // 2:
-            tail = pltpu.roll(tail, 64, 1)
-        rhs = jnp.concatenate([head, tail], axis=1)
-        rhs_v[p] = rhs
-        first = scale_v[p] * rhs
-        solution_v[p] = first
-        publish(0, p, first)
-        if p % 2 == 1:
-            send(0, p // 2)
-    wait_each(rhs_send, rhs_sems.at[0])
+    for q in range(3):
+        wait_each(rhs_land.at[:, q], rhs_sems.at[1, q])
+        total = rhs_own[q]
+        for s in range(8):
+            total += rhs_land[s, q].astype(F32)
+        tails = (total[32:48], pltpu.roll(total[32:48], 64, 1))
+        for half in range(2):
+            p = 2 * q + half
+            rhs = jnp.concatenate([total[16 * half : 16 * half + 16], tails[half]], axis=1)
+            rhs_v[p] = rhs
+            first = scale_v[p] * rhs
+            solution_v[p] = first
+            publish(0, p, first)
+        send(0, q)
+    for q in range(3):
+        wait_each(rhs_send.at[:, q], rhs_sems.at[0, q])
 
     for c in range(7, bricks):
         repack(c)
@@ -336,24 +333,37 @@
                 right = land[par, SLOT[e], p, 1].astype(F32)
                 joined[i, p] = jnp.where(low, pltpu.roll(left, 64, 1), right).astype(BF16)
 
-    def apply(par, c, columns, pairs_joined, at):
+    def inner_tiles(par, c, columns):
         p = c // 2
-        other = p - 1 if c % 2 == 0 else p + 1
         tiles = [column(par, d, p, 0) for d in columns]
         tiles += [column(par, d, p, 1) for d in columns]
-        tiles += [turned[d, p] for d in columns]
-        if c != 0 and c != bricks - 1:
-            tiles += [turned[d, other] for d in columns]
-            tiles += [joined[i, other] for i in pairs_joined]
+        return tiles + [turned[d, p] for d in columns]
+
+    def outer_tiles(c, columns, pairs_joined):
+        if c == 0 or c == bricks - 1:
+            return []
+        other = c // 2 - 1 if c % 2 == 0 else c // 2 + 1
+        return [turned[d, other] for d in columns] + [joined[i, other] for i in pairs_joined]
+
+    def multiply(c, at, tiles):
         depth = 128 * len(tiles)
-        return dot_nt(jnp.concatenate(tiles, axis=1), packed[c, :, at : at + depth])
+        return dot_nt(jnp.concatenate(tiles, axis=1), packed[c, :, 128 * at : 128 * at + depth])
 
     def apply_own(par, c):
-        return apply(par, c, [OWN], [len(JOINED)], 0)
+        return multiply(c, 0, inner_tiles(par, c, [OWN]) + outer_tiles(c, [OWN], [len(JOINED)]))
+
+    def neighbours_at(c):
+        return 3 if c == 0 or c == bricks - 1 else 5
+
+    def apply_inner(par, c):
+        return multiply(c, neighbours_at(c), inner_tiles(par, c, NEIGHBOURS))
+
+    def apply_outer(c):
+        return multiply(c, neighbours_at(c) + 24, outer_tiles(c, NEIGHBOURS, range(len(JOINED))))
 
     def apply_neighbours(par, c):
-        at = 3 if c == 0 or c == bricks - 1 else 5
-        return apply(par, c, NEIGHBOURS, range(len(JOINED)), 128 * at)
+        tiles = inner_tiles(par, c, NEIGHBOURS) + outer_tiles(c, NEIGHBOURS, range(len(JOINED)))
+        return multiply(c, neighbours_at(c), tiles)
 
     def step(e, carry):
         now = lax.rem(e, 2)
@@ -377,9 +387,14 @@
         for c in range(bricks):
             if c in ARRIVE:
                 q = ARRIVE.index(c)
+                if q > 0:
+                    keep(c, apply_inner(now, c), True)
                 wait_chunk(now, q, recv_sems)
                 expand(now, q)
-            keep(c, apply_neighbours(now, c), True)
+            if c in ARRIVE[1:]:
+                keep(c, apply_outer(c), True)
+            else:
+                keep(c, apply_neighbours(now, c), True)
             if c % 2 == 1:
                 finish(c // 2)
             if c in LEAVE:
@@ -393,7 +408,9 @@
     end = (SWEEPS - 1) % 2
     for p in range(pairs):
         for half in range(2):
-            coarse_ref[2 * p + half] = solution_v[p, 8 * half : 8 * half + loads, 0:values]
+            for l in range(loads):
+                row = 8 * half + l
+                coarse_ref[2 * p + half, l] = solution_v[p, row : row + 1, 0:values]
     for q in range(3):
         wait_chunk(end, q, recv_sems)
         wait_chunk(end, q, send_sems)
@@ -427,7 +444,7 @@
         kernel,
         out_shape=[
             jax.ShapeDtypeStruct((loads, values, slots), F32),
-            jax.ShapeDtypeStruct((bricks, loads, values), F32),
+            jax.ShapeDtypeStruct((bricks, loads, 1, values), F32),
         ],
         in_specs=[any_space] * 6,
         out_specs=[vmem, vmem],
@@ -444,9 +461,9 @@
             pltpu.VMEM((8, values, values), BF16),
             pltpu.VMEM((8, values, values), BF16),
             pltpu.VMEM((loads * slots, 9 * rows), BF16),
-            pltpu.VMEM((rows * 3 // 2, 128), F32),
-            pltpu.VMEM((8, rows * 3 // 2, 128), BF16),
-            pltpu.VMEM((8, rows * 3 // 2, 128), BF16),
+            pltpu.VMEM((3, 48, 128), F32),
+            pltpu.VMEM((8, 3, 48, 128), BF16),
+            pltpu.VMEM((8, 3, 48, 128), BF16),
             pltpu.VMEM((2, 8, pairs, 2, 16, 128), BF16),
             pltpu.VMEM((2, pairs, 2, 16, 128), BF16),
             pltpu.VMEM((9, pairs, 16, 128), BF16),
@@ -458,7 +475,7 @@
             dma((6,)),
             dma((bricks,)),
             dma,
-            dma((2,)),
+            dma((2, 3)),
             dma((2, 3)),
             dma((2, 3)),
         ]

time: 77.3 us -> 75.7 us (0.979)
  Pallas kernels: 72.8 us -> 71.4 us
    pallas_call x1, Pallas kernels: 72.8 us -> 71.4 us  [local(): pl.pallas_call(kernel, out_shape=[jax.ShapeDtypeStruct((loads, values, sl...]
where the time goes in v4:
time: 75.7 us; the launch traced here: 75.4 us
  Pallas kernels  71.4 us (94%)
  local copies, waits for them, and re-layouts  3.44 us (5%)
    pallas_call x1, Pallas kernels, local(): pl.pallas_call(kernel, out_shape=[jax.ShapeDtypeStruct((loads, values, sl...  71.4 us
    unnamed x2, local copies, waits for them, and re-layouts  3.44 us

profile of v4, /device:TPU:105, one launch (start us, length us, event | category | flops | bytes accessed | tf_op | source)
XLA Modules:
  0.0 75.4 jit_solution(2071176299378032455)
XLA Ops:
  0.6 71.4 %shard_map.77 = (f32[6,192,128]{2,1,0:T(8,128)}, f32[12,6,1,192]{3,2,1,0:T(1,128)}) custom-call(s32[1,128]{1,0:T(1,128)} %bitcast.15, s32[3,128]{1,0:T(4,128)} %bitcast.14, f32[6,192,128]{2,1,0:T(8,128)} %bitcast.11, f32[8,192,192]{2,1,0:T(8,128)} %restrict_hbm.1, bf16[12,27,192,192]{3,2,1,0:T(8,128)(2,1)} %bitcast.9, s32[12,1,26]{2,1,0:T(1,128)} %bitcast.13), custom_call_target="tpu_custom_call" | custom-call | tf_op jit(solution)/shard_map/pallas_call | solution.py:443
  72.0 1.9 %copy.11 = f32[128,6,192]{0,2,1:T(8,128)} copy(f32[128,6,192]{0,2,1:T(8,128)} %bitcast.10) | data formatting | bytes 1179648
  73.9 1.5 %copy.12 = f32[1,1,12,6,192]{4,1,3,2,0:T(1,128)} copy(f32[1,1,12,6,192]{4,1,3,2,0:T(1,128)} %bitcast.12) | data formatting | bytes 110592

commit v5 on v4

--- a/solution.py
+++ b/solution.py
@@ -13,7 +13,7 @@
 NEIGHBOURS = [d for d in range(9) if d != OWN]
 ARRIVE = (0, 3, 7)
 LEAVE = (4, 7, 11)
-AHEAD = 4
+AHEAD = 6
 SLOT = {d: (d if d < OWN else d - 1) for d in range(9) if d != OWN}
 JOINED = ((0, 1), (2, 3), (5, 6), (7, 8))
 NT = (((1,), (1,)), ((), ()))
@@ -411,6 +411,7 @@
             for l in range(loads):
                 row = 8 * half + l
                 coarse_ref[2 * p + half, l] = solution_v[p, row : row + 1, 0:values]
+    octant_up = jnp.concatenate([upright(octant)] * loads, axis=0)
     for q in range(3):
         wait_chunk(end, q, recv_sems)
         wait_chunk(end, q, send_sems)
@@ -423,7 +424,6 @@
         axis=0,
     )
     fetched = dot(gather_v[...], around)[:, 0:values].astype(BF16)
-    octant_up = jnp.concatenate([upright(octant)] * loads, axis=0)
     total = jnp.zeros((values, loads * slots), F32)
     for o in range(8):
         chosen = fetched * jnp.where(octant_up == o, 1.0, 0.0).astype(BF16)

time: 75.7 us -> 75.6 us (level)
  no operation moved by 1% of the time
where the time goes in v5:
time: 75.6 us; the launch traced here: 75.4 us
  Pallas kernels  71.4 us (94%)
  local copies, waits for them, and re-layouts  3.44 us (5%)
    pallas_call x1, Pallas kernels, local(): pl.pallas_call(kernel, out_shape=[jax.ShapeDtypeStruct((loads, values, sl...  71.4 us
    unnamed x2, local copies, waits for them, and re-layouts  3.44 us

profile of v5, /device:TPU:105, one launch (start us, length us, event | category | flops | bytes accessed | tf_op | source)
XLA Modules:
  0.0 75.4 jit_solution(5076394598195687583)
XLA Ops:
  0.6 71.4 %shard_map.77 = (f32[6,192,128]{2,1,0:T(8,128)}, f32[12,6,1,192]{3,2,1,0:T(1,128)}) custom-call(s32[1,128]{1,0:T(1,128)} %bitcast.15, s32[3,128]{1,0:T(4,128)} %bitcast.14, f32[6,192,128]{2,1,0:T(8,128)} %bitcast.11, f32[8,192,192]{2,1,0:T(8,128)} %restrict_hbm.1, bf16[12,27,192,192]{3,2,1,0:T(8,128)(2,1)} %bitcast.9, s32[12,1,26]{2,1,0:T(1,128)} %bitcast.13), custom_call_target="tpu_custom_call" | custom-call | tf_op jit(solution)/shard_map/pallas_call | solution.py:443
  72.0 1.9 %copy.11 = f32[128,6,192]{0,2,1:T(8,128)} copy(f32[128,6,192]{0,2,1:T(8,128)} %bitcast.10) | data formatting | bytes 1179648
  73.9 1.5 %copy.12 = f32[1,1,12,6,192]{4,1,3,2,0:T(1,128)} copy(f32[1,1,12,6,192]{4,1,3,2,0:T(1,128)} %bitcast.12) | data formatting | bytes 110592
